TPU v7x, 512 devices: a whole 4x8x8 slice. The times are simulated.
512 devices in a mesh: ctx: 64 (over z, y_lo, core), tp: 8 (over x, y_hi).
Axes of the slice: x: 4, y: 8 (y_hi: 2, y_lo: 4; y = y_hi * 4 + y_lo), z: 8, core: 2. Of those that a mesh axis runs over, the one named last changes fastest.
Arguments:
- hidden_in: bfloat16 [256, 8192], P('tp', 'ctx'), may hold values from -6 to 6
- w_query: bfloat16 [8192, 8192], P('ctx', 'tp'), may hold values from -0.1875 to 0.1875
- w_key: bfloat16 [8192, 1024], P('ctx', 'tp'), may hold values from -0.09375 to 0.09375
- w_value: bfloat16 [8192, 1024], P('ctx', 'tp'), may hold values from -0.09375 to 0.09375
- w_out: bfloat16 [8192, 8192], P('tp', 'ctx'), may hold values from -0.1875 to 0.1875
- cache_keys: bfloat16 [32768, 8, 128], P('ctx', 'tp'), may hold values from -512 to 512
- cache_values: bfloat16 [32768, 8, 128], P('ctx', 'tp'), may hold values from -6 to 6
- prefix_lengths: int32 [64], P('ctx'), may hold values from 1 to 512, as said below
Outputs:
- attention_out: float32 [256, 8192], P('tp', 'ctx')
Inputs may be any that keep to these rules, and one draw needn't show every extreme that they name: `prefix_lengths`: every shard but the last holds 256 to 512 positions, and at least one of them is full; the last holds 1 to 512.
All inputs are finite; a program needn't handle non-finite values.
Results may differ from a plain program's by a relative error of at most 0.0059.
The roundings to bfloat16 on the way count: a program that leaves them out, or rounds other values in their place, can miss the bound.
Values may be sent and summed in bfloat16 or wider, within the bound.
A program may use at most 192 MiB of HBM per device.

v0:
```python
import math

import jax
import jax.numpy as jnp
from jax import lax
from jax.sharding import PartitionSpec as P


def absorb(carried, queries, key_rows, value_rows, visible, factor):
    weighted, highest, totals = carried
    scores = (
        jnp.einsum("rgd,kd->rgk", queries, key_rows, preferred_element_type=jnp.float32) * factor
    )
    scores = jnp.where(visible, scores, -1e30)
    raised = jnp.maximum(highest, jnp.max(scores, axis=-1))
    shrink = jnp.exp(highest - raised)
    weights = jnp.exp(scores - raised[..., None])
    totals = totals * shrink + jnp.sum(weights, axis=-1)
    weighted = weighted * shrink[..., None] + jnp.einsum(
        "rgk,kd->rgd", weights.astype(jnp.bfloat16), value_rows, preferred_element_type=jnp.float32
    )
    return (weighted, raised, totals)


def per_device(hidden_in, w_query, w_key, w_value, w_out, cache_keys, cache_values, prefix_lengths):
    ctx_count = lax.axis_size("ctx")
    ctx_index = lax.axis_index("ctx")
    columns = lax.all_gather(hidden_in, "tp", axis=0, tiled=True)
    total_rows = columns.shape[0]
    own_rows = total_rows // ctx_count
    head_dim = w_key.shape[1]
    width = w_query.shape[1]
    group = width // head_dim
    factor = head_dim ** (-0.5)
    joined = jnp.concatenate([w_query, w_key, w_value], axis=1)
    projected = lax.psum_scatter(
        jnp.dot(columns, joined, preferred_element_type=jnp.float32),
        "ctx",
        scatter_dimension=0,
        tiled=True,
    )
    queries = projected[:, :width].astype(jnp.bfloat16).reshape(own_rows, group, head_dim)
    new_keys = projected[:, width : width + head_dim].astype(jnp.bfloat16)
    new_values = projected[:, width + head_dim :].astype(jnp.bfloat16)
    stored_keys = cache_keys[:, 0, :]
    stored_values = cache_values[:, 0, :]
    filled = prefix_lengths[0]
    shard_len = stored_keys.shape[0]
    block_len = math.gcd(shard_len, 512)
    block_count = shard_len // block_len
    key_blocks = stored_keys.reshape(block_count, block_len, head_dim)
    value_blocks = stored_values.reshape(block_count, block_len, head_dim)
    block_starts = jnp.arange(block_count, dtype=jnp.int32) * block_len
    offsets = jnp.arange(block_len, dtype=jnp.int32)
    own_positions = ctx_index * own_rows + jnp.arange(own_rows, dtype=jnp.int32)
    query_piece = lax.all_gather(queries, "ctx", axis=0, tiled=True)
    row_count = query_piece.shape[0]
    begin = (
        jnp.zeros((row_count, group, head_dim), jnp.float32),
        jnp.full((row_count, group), -1e30, jnp.float32),
        jnp.zeros((row_count, group), jnp.float32),
    )

    def visit_block(status, inputs):
        key_rows, value_rows, block_start = inputs
        visible = (block_start + offsets < filled)[None, None, :]
        return (absorb(status, query_piece, key_rows, value_rows, visible, factor), None)

    status, unused = lax.scan(visit_block, begin, (key_blocks, value_blocks, block_starts))
    query_positions = jnp.arange(row_count, dtype=jnp.int32)
    causal = (own_positions[None, :] <= query_positions[:, None])[:, None, :]
    status = absorb(status, query_piece, new_keys, new_values, causal, factor)
    weighted, highest, totals = tuple((portion for portion in status))
    got_weighted, got_highest, got_totals = (
        lax.all_to_all(weighted, "ctx", split_axis=0, concat_axis=0, tiled=True),
        lax.all_to_all(highest, "ctx", split_axis=0, concat_axis=0, tiled=True),
        lax.all_to_all(totals, "ctx", split_axis=0, concat_axis=0, tiled=True),
    )
    got_weighted = got_weighted.reshape(ctx_count, own_rows, group, head_dim)
    got_highest = got_highest.reshape(ctx_count, own_rows, group)
    got_totals = got_totals.reshape(ctx_count, own_rows, group)
    overall = jnp.max(got_highest, axis=0)
    shrink = jnp.exp(got_highest - overall)
    summed = jnp.sum(got_totals * shrink, axis=0)
    merged = jnp.sum(got_weighted * shrink[..., None], axis=0)
    attended = (merged / summed[..., None]).astype(jnp.bfloat16).reshape(own_rows, width)
    head_terms = jnp.dot(
        lax.all_gather(attended, "ctx", axis=0, tiled=True),
        w_out,
        preferred_element_type=jnp.float32,
    )
    return lax.psum_scatter(head_terms, "tp", scatter_dimension=0, tiled=True)


def solution(mesh):
    placed = (
        P("tp", "ctx"),
        P("ctx", "tp"),
        P("ctx", "tp"),
        P("ctx", "tp"),
        P("tp", "ctx"),
        P("ctx", "tp", None),
        P("ctx", "tp", None),
        P("ctx"),
    )
    return jax.shard_map(
        per_device, mesh=mesh, in_specs=placed, out_specs=P("tp", "ctx"), check_vma=False
    )
```

profile of v0, /device:TPU:1, one launch (start us, length us, event | category | flops | bytes accessed | tf_op | source)
XLA Modules:
  0.0 663.6 jit_solution(7143726004692121679)
XLA Ops:
  7.3 39.4 %all_gather.9 = bf16[256,128]{1,0:T(8,128)(2,1)S(1)} all-gather(bf16[32,128]{1,0:T(8,128)(2,1)} %param.8), channel_id=1, replica_groups=mesh['ctx'=64,'tp'=8] {'tp'}, dimensions={0}, use_global_device_ids=true | all-gather | bytes 73728 | tf_op jit(solution)/shard_map/all_gather | solution.py:28
  46.7 1.3 convolution_bitcast_fusion
  48.1 284.4 %all-reduce.2 = bf16[256,1280]{0,1:T(8,128)(2,1)S(1)} all-reduce(f32[256,1280]{0,1:T(8,128)S(1)} %convolution_bitcast_fusion), channel_id=2, replica_groups=mesh['ctx'=64,'tp'=8] {'ctx'}, use_global_device_ids=true, to_apply=%region_0.0.clone | all-reduce | flops 327680 | bytes 1966080
  332.5 1.3 dynamic-slice
  334.5 0.2 constant_dynamic-slice_fusion
  334.6 0.2 copy.45
  334.8 81.8 %all_gather.10 = bf16[256,8,128]{2,1,0:T(8,128)(2,1)S(1)} all-gather(bf16[4,8,128]{2,1,0:T(8,128)(2,1)S(1)} %bitcast.44), channel_id=1, replica_groups=mesh['ctx'=64,'tp'=8] {'ctx'}, dimensions={0}, use_global_device_ids=true | all-gather | bytes 532480 | tf_op jit(solution)/shard_map/all_gather | solution.py:56
  416.6 2.4 fusion.27
  419.0 0.2 copy.47
  419.3 0.1 copy.52
  419.4 2.7 fusion
  422.1 0.1 copy.51
  422.2 3.3 fusion.1
  425.5 0.1 copy.55
  425.7 0.1 copy.57
  425.8 0.8 multiply_add_fusion
  426.6 5.9 all-to-all-start.2
  432.5 3.1 fusion.9
  435.5 7.8 %all-to-all-done.2 = f32[64,4,8]{2,1,0:T(4,128)S(1)} async-done(((f32[64,4,8]{2,1,0:T(4,128)}), f32[64,4,8]{2,1,0:T(4,128)S(1)}, u32[]{:S(2)}, u32[]{:S(2)}) %all-to-all-start.2) | async-done | bytes 8224 | tf_op jit(solution)/shard_map/all_to_all | solution.py:77
  443.3 4.4 all-to-all-start.1
  447.7 0.4 convolution_add_fusion
  448.1 1.6 copy.50
  449.7 9.0 %all-to-all-done.1 = f32[64,4,8]{2,1,0:T(4,128)S(1)} async-done(((f32[64,4,8]{2,1,0:T(4,128)}), f32[64,4,8]{2,1,0:T(4,128)S(1)}, u32[]{:S(2)}, u32[]{:S(2)}) %all-to-all-start.1) | async-done | bytes 8224 | tf_op jit(solution)/shard_map/all_to_all | solution.py:76
  458.7 4.5 all-to-all-start
  463.3 0.1 multiply_reduce_fusion
  463.5 0.5 copy.53
  463.9 27.8 %all-to-all-done = f32[256,8,128]{2,1,0:T(8,128)S(1)} async-done(((f32[256,8,128]{2,1,0:T(8,128)}), f32[256,8,128]{2,1,0:T(8,128)S(1)}, u32[]{:S(2)}, u32[]{:S(2)}) %all-to-all-start) | async-done | bytes 1048608 | tf_op jit(solution)/shard_map/all_to_all | solution.py:75
  491.8 0.7 fusion.12
  492.6 78.6 %all-gather = bf16[64,4,1024]{2,1,0:T(4,128)(2,1)S(1)} all-gather(bf16[1,4,1024]{2,1,0:T(4,128)(2,1)S(1)} %fusion.26), channel_id=1, replica_groups=mesh['ctx'=64,'tp'=8] {'ctx'}, dimensions={0}, use_global_device_ids=true | all-gather | bytes 532480 | tf_op jit(solution)/shard_map/all_gather | solution.py:88
  571.1 0.1 reshape.82
  571.3 0.9 fusion.32
  572.2 84.6 %reduce-scatter.3.cloned.1.call-done = f32[32,128]{1,0:T(8,128)} async-done(((f32[256,128]{1,0:T(8,128)}), f32[32,128]{1,0:T(8,128)}) %reduce-scatter.3.cloned.1.call-update) | async-done | bytes 16400 | tf_op jit(solution)/shard_map/reduce_scatter | solution.py:92
  (19 shorter events, 0.5 us)
Async XLA Ops:
  6.5 564.7 %copy-start = (bf16[1024,128]{1,0:T(8,128)(2,1)S(1)}, bf16[1024,128]{1,0:T(8,128)(2,1)}, u32[]{:S(2)}) copy-start(bf16[1024,128]{1,0:T(8,128)(2,1)} %param.12) | copy-start | bytes 786436
  6.5 412.8 %copy-start.1 = (bf16[512,1,128]{2,0,1:T(8,128)(2,1)S(1)}, bf16[512,1,128]{2,0,1:T(8,128)(2,1)}, u32[]{:S(2)}) copy-start(bf16[512,1,128]{2,0,1:T(8,128)(2,1)} %param.13) | copy-start | bytes 393220
  419.4 13.1 %copy-start.2 = (bf16[512,1,128]{2,0,1:T(8,128)(2,1)S(1)}, bf16[512,1,128]{2,0,1:T(8,128)(2,1)}, u32[]{:S(2)}) copy-start(bf16[512,1,128]{2,0,1:T(8,128)(2,1)} %param.14) | copy-start | bytes 393220
  426.6 16.7 %all-to-all-start.2 = ((f32[64,4,8]{2,1,0:T(4,128)}), f32[64,4,8]{2,1,0:T(4,128)S(1)}, u32[]{:S(2)}, u32[]{:S(2)}) async-start(f32[64,4,8]{2,1,0:T(4,128)} %get-tuple-element.23), calls=%async_computation.2 | async-start | bytes 262144 | tf_op jit(solution)/shard_map/all_to_all | solution.py:77
  443.3 15.4 %all-to-all-start.1 = ((f32[64,4,8]{2,1,0:T(4,128)}), f32[64,4,8]{2,1,0:T(4,128)S(1)}, u32[]{:S(2)}, u32[]{:S(2)}) async-start(f32[64,4,8]{2,1,0:T(4,128)} %get-tuple-element.24), calls=%async_computation.1 | async-start | bytes 262144 | tf_op jit(solution)/shard_map/all_to_all | solution.py:76
  458.7 33.1 %all-to-all-start = ((f32[256,8,128]{2,1,0:T(8,128)}), f32[256,8,128]{2,1,0:T(8,128)S(1)}, u32[]{:S(2)}, u32[]{:S(2)}) async-start(f32[256,8,128]{2,1,0:T(8,128)} %copy.50), calls=%async_computation | async-start | bytes 2097152 | tf_op jit(solution)/shard_map/all_to_all | solution.py:75
  463.2 193.6 %reduce-scatter.3.cloned.1.call-start = ((), (), s32[]{:S(2)}) async-start(), calls=%async_computation.4 | async-start | bytes 147456 | tf_op jit(solution)/shard_map/reduce_scatter | solution.py:92
Sparse Core Ops, SparseCore 0:
  572.3 84.4 reduce-scatter.2
where the time goes:
time: 665 us; the launch traced here: 664 us
  blocking collectives  484 us (73%)
  waiting for transfers between devices  129 us (19%)
  between operations  15 us (2%)
  starting transfers between devices  14.8 us (2%)
  matrix products  10.7 us (2%)
    unnamed x1, blocking collectives  284 us
    reduce_scatter x1, waiting for transfers between devices, per_device(): return lax.psum_scatter(head_terms, 'tp', scatter_dimension=0, tiled=True)  84.6 us
    all_gather x1, blocking collectives, per_device(): query_piece = lax.all_gather(queries, 'ctx', axis=0, tiled=True)  81.8 us
    all_gather x1, blocking collectives, per_device(): lax.all_gather(attended, 'ctx', axis=0, tiled=True)  78.6 us
    all_gather x1, blocking collectives, per_device(): columns = lax.all_gather(hidden_in, 'tp', axis=0, tiled=True)  39.4 us
    all_to_all x1, waiting for transfers between devices, per_device(): lax.all_to_all(weighted, 'ctx', split_axis=0, concat_axis=0, tiled=True)  27.8 us
  transfers between devices with their start and end apart: 4, of which 4 were waited for; matrix products, arithmetic and copies ran while one was open for 1% of the time, Pallas kernels for 0%

commit v1 on v0

v1 whole, which is shorter than its diff:
```python
import functools
import math

import jax
import jax.numpy as jnp
from jax import lax
from jax.experimental import pallas as pl
from jax.experimental.pallas import tpu as pltpu
from jax.sharding import PartitionSpec as P

MESH = pl.DeviceIdType.MESH
F32 = jnp.float32
BF16 = jnp.bfloat16
NZ, NY, NX, NH = 8, 4, 4, 2
LOG2E = 1.0 / math.log(2.0)
NEG = -1e30


def coords():
    c = lax.axis_index("ctx")
    t = lax.axis_index("tp")
    return c // 8, (c // 2) % 4, c % 2, t // 2, t % 2


def device(z, y, core, x, h):
    return ((z * NY + y) * 2 + core, x * NH + h)


def dot(a, b):
    return jnp.dot(a, b, preferred_element_type=F32)


def dot_t(a, b):
    return lax.dot_general(a, b, (((1,), (1,)), ((), ())), preferred_element_type=F32)


def kernel(
    hid_ref, wq_ref, wk_ref, wv_ref, wo_ref, ck_ref, cv_ref, len_ref, out_ref,
    hs, wq, wkv, wo, kb, vb, yp, yin, kvs, kvin, p2s, p2d, qb, msgs, m_s, l_s, acc,
    po, pl_s, pod, pld, att, o2s, p7,
    loc, s_hy, r_hy, s_hx, r_hx, s_w, r_w, s_wo, r_wo, s_kc, r_kc, s_ky, r_ky, s_kr, r_kr,
    s_pc, r_pc, s_p2, r_p2, s_p3, r_p3, s_m, r_m, s_p5, r_p5, s_p6, r_p6, s_rc, r_rc, s_p7, r_p7,
):
    z, y, core, x, h = coords()
    other = 1 - core
    yf = h * NY + y
    tp = x * NH + h
    mine = y * 2 + core

    def remote(src, dst, ssem, rsem, dev):
        return pltpu.make_async_remote_copy(
            src_ref=src, dst_ref=dst, send_sem=ssem, recv_sem=rsem, device_id=dev, device_id_type=MESH
        )

    sends = []

    local = [
        pltpu.make_async_copy(wq_ref.at[:, pl.ds(pl.multiple_of(y * 256, 256), 256)], wq.at[y], loc.at[0]),
        pltpu.make_async_copy(wo_ref.at[pl.ds(pl.multiple_of(y * 256, 256), 256)], wo.at[y], loc.at[1]),
        pltpu.make_async_copy(ck_ref, kb.at[mine], loc.at[2]),
        pltpu.make_async_copy(cv_ref, vb.at[mine], loc.at[3]),
    ]
    for copy in local:
        copy.start()

    barrier = pltpu.get_barrier_semaphore()

    def greet(i, carry):
        dev = device(z, lax.rem(y + i % 4, 4), core, lax.rem(x + i // 8, 4), lax.rem(h + (i // 4) % 2, 2))
        pl.semaphore_signal(barrier, inc=1, device_id=dev, device_id_type=MESH)
        return carry

    lax.fori_loop(1, 32, greet, 0)
    for d in range(1, NZ):
        pl.semaphore_signal(
            barrier, inc=1, device_id=device(lax.rem(z + d, NZ), y, core, x, h), device_id_type=MESH
        )
    for d in range(NY):
        pl.semaphore_signal(
            barrier, inc=1, device_id=device(z, lax.rem(y + d, NY), other, x, h), device_id_type=MESH
        )
    pl.semaphore_wait(barrier, 31 + NZ - 1 + NY)

    own_rows = pl.ds(pl.multiple_of(tp * 32, 32), 32)
    own_cols = pl.ds(pl.multiple_of(y * 128, 128), 128)

    def hid_y(d):
        to = lax.rem(yf + d, 8)
        return remote(hid_ref, hs.at[own_rows, own_cols], s_hy.at[d], r_hy.at[d], device(z, to % 4, core, x, to // 4))

    for d in range(1, 8):
        copy = hid_y(d)
        copy.start()
        sends.append(copy)
    hs[own_rows, own_cols] = hid_ref[...]

    def weights(d):
        to = lax.rem(y + d, NY)
        dev = device(z, to, core, x, h)
        first = remote(
            wq_ref.at[:, pl.ds(pl.multiple_of(to * 256, 256), 256)], wq.at[y], s_w.at[0, d], r_w.at[0, d], dev
        )
        return first, to, dev

    def weights_kv(ref, d, dev):
        return remote(ref, wkv.at[y], s_w.at[1, d], r_w.at[1, d], dev)

    for d in range(1, NY):
        first, to, dev = weights(d)
        first.start()
        sends.append(first)

        @pl.when(to % 2 == 0)
        def _():
            weights_kv(wk_ref, d, dev).start()

        @pl.when(to % 2 == 1)
        def _():
            weights_kv(wv_ref, d, dev).start()

        sends.append(weights_kv(wk_ref, d, dev))

    @pl.when(y % 2 == 0)
    def _():
        wkv[y] = wk_ref[...]

    @pl.when(y % 2 == 1)
    def _():
        wkv[y] = wv_ref[...]

    twin = device(z, y, other, x, h)
    for i, (ref, buf) in enumerate(((ck_ref, kb), (cv_ref, vb))):
        copy = remote(ref, buf.at[mine], s_kc.at[i], r_kc.at[i], twin)
        copy.start()
        sends.append(copy)

    for d in range(1, 8):
        hid_y(d).wait_recv()

    def hid_x(d):
        rows = pl.ds(pl.multiple_of(x * 64, 64), 64)
        return remote(hs.at[rows], hs.at[rows], s_hx.at[d], r_hx.at[d], device(z, y, core, lax.rem(x + d, NX), h))

    for d in range(1, NX):
        copy = hid_x(d)
        copy.start()
        sends.append(copy)

    for d in range(1, NY):
        first, to, dev = weights(d)
        first.wait_recv()
        weights_kv(wk_ref, d, dev).wait_recv()
    local[0].wait()

    def cache_y(d, i):
        ref, buf = ((ck_ref, kb), (cv_ref, vb))[i]
        return remote(ref, buf.at[mine], s_ky.at[i, d], r_ky.at[i, d], device(z, lax.rem(y + d, NY), core, x, h))

    for d in (1, 3, 2):
        for i in range(2):
            copy = cache_y(d, i)
            copy.start()
            sends.append(copy)

    def out_weights(d):
        to = lax.rem(y + d, NY)
        return remote(
            wo_ref.at[pl.ds(pl.multiple_of(to * 256, 256), 256)], wo.at[y], s_wo.at[d], r_wo.at[d],
            device(z, to, core, x, h),
        )

    for d in range(1, NY):
        copy = out_weights(d)
        copy.start()
        sends.append(copy)

    wqf = wq[...].reshape(512, 256)
    wkvf = wkv[...].reshape(512, 128)

    def project(block):
        rows = pl.ds(pl.multiple_of(block * 64, 64), 64)
        part = hs[rows, :]
        both = dot(part, wqf)
        yp[0, rows, :] = both[:, :128]
        yp[1, rows, :] = both[:, 128:]
        yp[2, rows, :] = dot(part, wkvf)

    project(x)
    for d in range(1, NX):
        hid_x(d).wait_recv()
        project(lax.rem(x + NX - d, NX))

    half = 16 * (y // 2)
    for b in range(NZ):
        kvs[b] = yp[2, pl.ds(pl.multiple_of(32 * b + half + 8 * other, 8), 8), :]
    pair = [
        remote(yp.at[other], yin, s_pc.at[0], r_pc.at[0], twin),
        remote(kvs, kvin, s_pc.at[1], r_pc.at[1], twin),
    ]
    for copy in pair:
        copy.start()
        sends.append(copy)
    for copy in pair:
        copy.wait_recv()
    for b in range(NZ):
        rows = slice(32 * b, 32 * b + 32)
        p2s[b, 0:32, :] = yp[core, rows, :] + yin[rows, :]
        p2s[b, 32:40, :] = yp[2, pl.ds(pl.multiple_of(32 * b + half + 8 * core, 8), 8), :] + kvin[b]

    def zdev(d):
        to = lax.rem(z + d, NZ)
        return to, device(to, y, core, x, h)

    def p2(d):
        to, dev = zdev(d)
        return remote(p2s.at[to], p2d.at[z], s_p2.at[d], r_p2.at[d], dev)

    for d in range(1, NZ):
        copy = p2(d)
        copy.start()
        sends.append(copy)
    p2d[z] = p2s[z]
    for d in range(1, NZ):
        p2(d).wait_recv()
    total = p2d[0]
    for b in range(1, NZ):
        total = total + p2d[b]
    zrows = pl.ds(pl.multiple_of(z * 32, 32), 32)
    qb[zrows, :] = total[:32].astype(BF16)

    def p3(d):
        to, dev = zdev(d)
        return remote(qb.at[zrows], qb.at[zrows], s_p3.at[d], r_p3.at[d], dev)

    for d in range(1, NZ):
        copy = p3(d)
        copy.start()
        sends.append(copy)

    msgs[mine, 0:8, :] = total[32:]
    msgs[mine, 8:16, :] = jnp.full((8, 128), len_ref[0].astype(F32), F32)

    def message(d, k):
        dev = device(z, lax.rem(y + d, NY), lax.rem(core + k, 2), x, h)
        return remote(msgs.at[mine], msgs.at[mine], s_m.at[k, d], r_m.at[k, d], dev)

    line = [(d, k) for d in range(NY) for k in range(2) if (d, k) != (0, 0)]
    for d, k in line:
        copy = message(d, k)
        copy.start()
        sends.append(copy)
    for d, k in line:
        message(d, k).wait_recv()
    for d in range(1, NZ):
        p3(d).wait_recv()

    scale = LOG2E / math.sqrt(128.0)
    queries = qb[...]
    m_s[...] = jnp.full((256, 1), NEG, F32)
    l_s[...] = jnp.zeros((256, 1), F32)
    acc[...] = jnp.zeros((256, 128), F32)

    def absorb(scores, values):
        before = m_s[...]
        raised = jnp.maximum(before, jnp.max(scores, axis=1, keepdims=True))
        shrink = jnp.exp2(before - raised)
        weight = jnp.exp2(scores - raised)
        l_s[...] = l_s[...] * shrink + jnp.sum(weight, axis=1, keepdims=True)
        acc[...] = acc[...] * shrink + dot(weight.astype(BF16), values)
        m_s[...] = raised

    def shard(index):
        filled = jnp.concatenate([msgs[index, 8:9, :]] * 4, axis=1)
        place = lax.broadcasted_iota(jnp.int32, (1, 512), 1).astype(F32)
        bias = jnp.where(place < filled, 0.0, NEG)
        absorb(dot_t(queries, kb[index]) * scale + bias, vb[index])

    def relay(d, i):
        index = lax.rem(y + NY - d, NY) * 2 + core
        buf = (kb, vb)[i]
        return remote(buf.at[index], buf.at[index], s_kr.at[i, d], r_kr.at[i, d], twin)

    local[2].wait()
    local[3].wait()
    shard(mine)
    for i, (ref, buf) in enumerate(((ck_ref, kb), (cv_ref, vb))):
        remote(ref, buf.at[mine], s_kc.at[i], r_kc.at[i], twin).wait_recv()
    shard(y * 2 + other)

    new_keys = jnp.concatenate([msgs[i, 0:8, :] for i in (0, 1, 4, 5)], axis=0).astype(BF16)
    new_values = jnp.concatenate([msgs[i, 0:8, :] for i in (2, 3, 6, 7)], axis=0).astype(BF16)
    key_at = lax.broadcasted_iota(jnp.int32, (256, 32), 1) + z * 32
    row_at = lax.broadcasted_iota(jnp.int32, (256, 32), 0)
    absorb(jnp.where(key_at <= row_at, dot_t(queries, new_keys) * scale, NEG), new_values)

    for d in (1, 3, 2):
        for i in range(2):
            cache_y(d, i).wait_recv()
            copy = relay(d, i)
            copy.start()
            sends.append(copy)
        shard(lax.rem(y + NY - d, NY) * 2 + core)
        for i in range(2):
            relay(d, i).wait_recv()
        shard(lax.rem(y + NY - d, NY) * 2 + other)

    sums = l_s[...]
    po[...] = (acc[...] / sums).astype(BF16)
    level = m_s[...] + jnp.log2(sums)
    diagonal = lax.broadcasted_iota(jnp.int32, (32, 128), 0) == lax.broadcasted_iota(jnp.int32, (32, 128), 1)
    for b in range(NZ):
        spread = jnp.where(diagonal, level[32 * b : 32 * b + 32], 0.0)
        pl_s[b] = jnp.broadcast_to(jnp.sum(spread, axis=0, keepdims=True), (8, 128))

    def p5(d, i):
        to, dev = zdev(d)
        if i == 0:
            rows = pl.ds(pl.multiple_of(to * 32, 32), 32)
            return remote(po.at[rows], pod.at[z], s_p5.at[0, d], r_p5.at[0, d], dev)
        return remote(pl_s.at[to], pld.at[z], s_p5.at[1, d], r_p5.at[1, d], dev)

    for d in range(1, NZ):
        for i in range(2):
            copy = p5(d, i)
            copy.start()
            sends.append(copy)
    pod[z] = po[zrows, :]
    pld[z] = pl_s[z]
    for d in range(1, NZ):
        for i in range(2):
            p5(d, i).wait_recv()

    levels = []
    for b in range(NZ):
        spread = jnp.where(diagonal, jnp.broadcast_to(pld[b, 0:1, :], (32, 128)), 0.0)
        levels.append(jnp.sum(spread, axis=1, keepdims=True))
    top = functools.reduce(jnp.maximum, levels)
    shares = [jnp.exp2(level_b - top) for level_b in levels]
    whole = functools.reduce(jnp.add, shares)
    merged = functools.reduce(jnp.add, [pod[b].astype(F32) * shares[b] for b in range(NZ)])
    att[0, zrows, :] = (merged / whole).astype(BF16)

    def p6(d):
        to, dev = zdev(d)
        return remote(att.at[0, zrows], att.at[0, zrows], s_p6.at[d], r_p6.at[d], dev)

    for d in range(1, NZ):
        copy = p6(d)
        copy.start()
        sends.append(copy)
    for d in range(1, NZ):
        p6(d).wait_recv()
    across = remote(att.at[0], att.at[1], s_rc, r_rc, twin)
    across.start()
    sends.append(across)

    local[1].wait()
    for d in range(1, NY):
        out_weights(d).wait_recv()
    head_rows = pl.ds(pl.multiple_of(core * 128, 128), 128)
    twin_rows = pl.ds(pl.multiple_of(other * 128, 128), 128)
    first = [dot(att[0], wo[b, head_rows, :]) for b in range(NY)]
    across.wait_recv()
    for b in range(NY):
        o2s[b] = (first[b] + dot(att[1], wo[b, twin_rows, :])).astype(BF16)

    def p7_copy(i):
        ty, tx, th = lax.rem(y + i % 4, 4), lax.rem(x + i // 8, 4), lax.rem(h + (i // 4) % 2, 2)
        rows = pl.ds(pl.multiple_of((tx * NH + th) * 32, 32), 32)
        return remote(
            o2s.at[ty, rows], p7.at[tp * NY + y], s_p7.at[i], r_p7.at[i], device(z, ty, core, tx, th)
        )

    def p7_start(i, carry):
        p7_copy(i).start()
        return carry

    def p7_recv(i, carry):
        p7_copy(i).wait_recv()
        return carry

    def p7_send(i, carry):
        p7_copy(i).wait_send()
        return carry

    lax.fori_loop(1, 32, p7_start, 0)
    p7[tp * NY + y] = o2s[y, own_rows, :]
    lax.fori_loop(1, 32, p7_recv, 0)
    result = p7[0].astype(F32)
    for b in range(1, 32):
        result = result + p7[b].astype(F32)
    out_ref[...] = result

    for copy in sends:
        copy.wait_send()
    lax.fori_loop(1, 32, p7_send, 0)


def per_device(hidden_in, w_query, w_key, w_value, w_out, cache_keys, cache_values, prefix_lengths):
    dma = pltpu.SemaphoreType.DMA
    vmem = pltpu.VMEM
    in_vmem = pl.BlockSpec(memory_space=pltpu.VMEM)
    anywhere = pl.BlockSpec(memory_space=pl.ANY)
    return pl.pallas_call(
        kernel,
        out_shape=jax.ShapeDtypeStruct((32, 128), F32),
        in_specs=[in_vmem, anywhere, in_vmem, in_vmem, anywhere, anywhere, anywhere,
                  pl.BlockSpec(memory_space=pltpu.SMEM)],
        out_specs=in_vmem,
        scratch_shapes=[
            vmem((256, 512), BF16), vmem((4, 128, 256), BF16), vmem((4, 128, 128), BF16),
            vmem((4, 256, 128), BF16), vmem((8, 512, 128), BF16), vmem((8, 512, 128), BF16),
            vmem((3, 256, 128), F32), vmem((256, 128), F32), vmem((8, 8, 128), F32), vmem((8, 8, 128), F32),
            vmem((8, 40, 128), F32), vmem((8, 40, 128), F32), vmem((256, 128), BF16), vmem((8, 16, 128), F32),
            vmem((256, 1), F32), vmem((256, 1), F32), vmem((256, 128), F32),
            vmem((256, 128), BF16), vmem((8, 8, 128), F32), vmem((8, 32, 128), BF16), vmem((8, 8, 128), F32),
            vmem((2, 256, 128), BF16), vmem((4, 256, 128), BF16), vmem((32, 32, 128), BF16),
            dma((4,)), dma((8,)), dma((8,)), dma((4,)), dma((4,)), dma((2, 4)), dma((2, 4)), dma((4,)), dma((4,)),
            dma((2,)), dma((2,)), dma((2, 4)), dma((2, 4)), dma((2, 4)), dma((2, 4)),
            dma((2,)), dma((2,)), dma((8,)), dma((8,)), dma((8,)), dma((8,)), dma((2, 4)), dma((2, 4)),
            dma((2, 8)), dma((2, 8)), dma((8,)), dma((8,)), dma, dma, dma((32,)), dma((32,)),
        ],
        compiler_params=pltpu.CompilerParams(
            collective_id=0, has_side_effects=True, vmem_limit_bytes=40 * 1024 * 1024
        ),
        cost_estimate=pl.CostEstimate(flops=1_000_000_000, bytes_accessed=2_000_000, transcendentals=1_100_000),
        name="attention_block",
    )(
        hidden_in, w_query, w_key, w_value, w_out,
        cache_keys.reshape(cache_keys.shape[0], 128), cache_values.reshape(cache_values.shape[0], 128),
        prefix_lengths,
    )


def solution(mesh):
    placed = (
        P("tp", "ctx"),
        P("ctx", "tp"),
        P("ctx", "tp"),
        P("ctx", "tp"),
        P("tp", "ctx"),
        P("ctx", "tp", None),
        P("ctx", "tp", None),
        P("ctx"),
    )
    return jax.shard_map(
        per_device, mesh=mesh, in_specs=placed, out_specs=P("tp", "ctx"), check_vma=False
    )
```

time: 665 us -> 95.6 us (0.14)
  blocking collectives: 484 us -> 0 us
  waiting for transfers between devices: 129 us -> 0 us
  Pallas kernels: 0 us -> 88 us
  starting transfers between devices: 14.8 us -> 0 us
  between operations: 15 us -> 0.67 us
  matrix products: 10.7 us -> 0 us
    unnamed x1 -> x0, blocking collectives: 284 us -> none
    all_gather x3 -> x0, blocking collectives: 200 us -> none  [the longest x1 81.8 us: per_device(): query_piece = lax.all_gather(queries, 'ctx', axis=0, tiled=True)]
    pallas_call x0 -> x1, Pallas kernels: none -> 88 us  [per_device(): pl.pallas_call(kernel, out_shape=jax.ShapeDtypeStruct((32, 128), F32), in...]
    reduce_scatter x1 -> x0, waiting for transfers between devices: 84.6 us -> none  [per_device(): return lax.psum_scatter(head_terms, 'tp', scatter_dimension=0, tiled=True)]
    all_to_all x3 -> x0, waiting for transfers between devices: 44.6 us -> none  [the longest x1 27.8 us: per_device(): lax.all_to_all(weighted, 'ctx', split_axis=0, concat_axis=0, tiled=True)]
    all_to_all x3 -> x0, starting transfers between devices: 14.8 us -> none  [the longest x1 5.85 us: per_device(): lax.all_to_all(totals, 'ctx', split_axis=0, concat_axis=0, tiled=True)]
    dot_general x6 -> x0, matrix products: 10.7 us -> none  [the longest x2 5.05 us: absorb(): jnp.einsum('rgd,kd->rgk', queries, key_rows, preferred_element_type=jnp.f...]
  transfers between devices with their start and end apart: 4 -> 0, of which waited for: 4 -> 0; matrix products, arithmetic and copies ran while one was open for 1% -> 0% of each run, Pallas kernels for 0% -> 0%
where the time goes in v1:
time: 95.6 us; the launch traced here: 95.2 us
  Pallas kernels  88 us (92%)
  local copies, waits for them, and re-layouts  6.52 us (7%)
    pallas_call x1, Pallas kernels, per_device(): pl.pallas_call(kernel, out_shape=jax.ShapeDtypeStruct((32, 128), F32), in...  88 us
    unnamed x15, local copies, waits for them, and re-layouts  6.52 us

profile of v1, /device:TPU:1, one launch (start us, length us, event | category | flops | bytes accessed | tf_op | source)
XLA Modules:
  0.0 95.2 jit_solution(14715446484961408354)
XLA Ops:
  0.7 0.0 copy-start
  0.7 0.9 copy-done
  1.6 0.0 copy-start.1
  1.6 0.9 copy-done.1
  2.6 0.0 copy-start.2
  2.6 0.9 copy-done.2
  3.5 0.0 copy-start.3
  3.5 0.9 copy-done.3
  4.4 0.0 copy-start.4
  4.4 0.8 copy-done.4
  5.1 0.0 copy-start.5
  5.1 0.8 copy-done.5
  5.9 0.0 copy-start.6
  5.9 0.7 copy-done.6
  6.6 88.0 %attention_block.1 = f32[32,128]{1,0:T(8,128)S(1)} custom-call(bf16[32,128]{1,0:T(8,128)(2,1)S(1)} %copy-done.6, bf16[128,1024]{1,0:T(8,128)(2,1)S(1)} %copy-done, bf16[128,128]{1,0:T(8,128)(2,1)S(1)} %copy-done.4, bf16[128,128]{1,0:T(8,128)(2,1)S(1)} %copy-done.5, bf16[1024,128]{1,0:T(8,128)(2,1)S(1)} %copy-done.1, bf16[512,128]{1,0:T(8,128)(2,1)S(1)} %bitcast.2, ...), custom_call_target="tpu_custom_call" | custom-call | flops 1000000000 | bytes 2000000 | tf_op jit(solution)/shard_map/attention_block/pallas_call | solution.py:404
  94.6 0.6 copy.11
Async XLA Ops:
  0.7 1.0 copy-start
  1.6 0.9 copy-start.1
  2.6 0.9 copy-start.2
  3.5 0.9 copy-start.3
  4.4 0.8 copy-start.4
  5.1 0.8 copy-start.5
  5.9 0.7 copy-start.6

commit v2 on v1

v2 whole, which is shorter than its diff:
```python
import functools
import math

import jax
import jax.numpy as jnp
from jax import lax
from jax.experimental import pallas as pl
from jax.experimental.pallas import tpu as pltpu
from jax.sharding import PartitionSpec as P

MESH = pl.DeviceIdType.MESH
F32 = jnp.float32
BF16 = jnp.bfloat16
NZ, NY, NX, NH = 8, 4, 4, 2
LOG2E = 1.0 / math.log(2.0)
NEG = -1e30
KEYS_WITH = 1
HEADS_WITH = 2


def coords():
    c = lax.axis_index("ctx")
    t = lax.axis_index("tp")
    return c // 8, (c // 2) % 4, c % 2, t // 2, t % 2


def device(z, y, core, x, h):
    return ((z * NY + y) * 2 + core, x * NH + h)


def dot(a, b):
    return jnp.dot(a, b, preferred_element_type=F32)


def dot_t(a, b):
    return lax.dot_general(a, b, (((1,), (1,)), ((), ())), preferred_element_type=F32)


def kernel(
    hid_ref, wq_ref, wk_ref, wv_ref, wo_ref, ck_ref, cv_ref, len_ref, out_ref,
    hs, wqs, wkvs, wos, wq, wkv, wo, kb, vb, yp, yin, kvs, kvin, p2s, p2d, qb, msgs, m_s, l_s, acc,
    po, pod, att, o2s, p7,
    loc, s_hy, r_hy, s_hx, r_hx, s_w, r_w, s_wo, r_wo, s_kc, r_kc, s_ky, r_ky, s_kr, r_kr,
    s_pc, r_pc, s_p2, r_p2, s_p3, r_p3, s_m, r_m, s_p5, r_p5, s_p6, r_p6, s_rc, r_rc, s_p7, r_p7,
):
    z, y, core, x, h = coords()
    other = 1 - core
    yf = h * NY + y
    tp = x * NH + h
    mine = y * 2 + core
    own_rows = pl.ds(pl.multiple_of(tp * 32, 32), 32)
    own_cols = pl.ds(pl.multiple_of(y * 128, 128), 128)

    def xor_y(bits):
        if bits == 1:
            return y + 1 - 2 * (y % 2)
        return lax.rem(y + 2, NY)

    keys_y, heads_y = xor_y(KEYS_WITH), xor_y(HEADS_WITH)

    def remote(src, dst, ssem, rsem, dev):
        return pltpu.make_async_remote_copy(
            src_ref=src, dst_ref=dst, send_sem=ssem, recv_sem=rsem, device_id=dev, device_id_type=MESH
        )

    sends = []

    local = [
        pltpu.make_async_copy(hid_ref, hs.at[own_rows, own_cols], loc.at[0]),
        pltpu.make_async_copy(wq_ref, wqs, loc.at[1]),
        pltpu.make_async_copy(wk_ref, wkvs.at[0], loc.at[2]),
        pltpu.make_async_copy(wv_ref, wkvs.at[1], loc.at[3]),
        pltpu.make_async_copy(ck_ref, kb.at[mine], loc.at[4]),
        pltpu.make_async_copy(cv_ref, vb.at[mine], loc.at[5]),
        pltpu.make_async_copy(wo_ref, wos, loc.at[6]),
    ]
    for copy in local:
        copy.start()

    barrier = pltpu.get_barrier_semaphore()

    def greet(i, carry):
        dev = device(z, lax.rem(y + i % 4, 4), core, lax.rem(x + i // 8, 4), lax.rem(h + (i // 4) % 2, 2))
        pl.semaphore_signal(barrier, inc=1, device_id=dev, device_id_type=MESH)
        return carry

    lax.fori_loop(1, 32, greet, 0)
    for d in range(1, NZ):
        pl.semaphore_signal(
            barrier, inc=1, device_id=device(lax.rem(z + d, NZ), y, core, x, h), device_id_type=MESH
        )
        pl.semaphore_signal(
            barrier, inc=1, device_id=device(lax.rem(z + d, NZ), heads_y, core, x, h), device_id_type=MESH
        )
    for d in range(NY):
        pl.semaphore_signal(
            barrier, inc=1, device_id=device(z, lax.rem(y + d, NY), other, x, h), device_id_type=MESH
        )
    pl.semaphore_wait(barrier, 31 + 2 * (NZ - 1) + NY)

    own_hidden = hs.at[own_rows, own_cols]

    def hid_y(d):
        to = lax.rem(yf + d, 8)
        return remote(own_hidden, own_hidden, s_hy.at[d], r_hy.at[d], device(z, to % 4, core, x, to // 4))

    local[0].wait()
    for d in range(1, 8):
        copy = hid_y(d)
        copy.start()
        sends.append(copy)

    def weights(d, i):
        to = lax.rem(y + d, NY)
        dev = device(z, to, core, x, h)
        if i == 0:
            part = wqs.at[:, pl.ds(pl.multiple_of(to * 256, 256), 256)]
            return remote(part, wq.at[y], s_w.at[0, d], r_w.at[0, d], dev)
        return remote(wkvs.at[to % 2], wkv.at[y], s_w.at[1, d], r_w.at[1, d], dev)

    for copy in local[1:4]:
        copy.wait()
    for d in range(1, NY):
        for i in range(2):
            copy = weights(d, i)
            copy.start()
            sends.append(copy)
    wq[y] = wqs[:, pl.ds(pl.multiple_of(y * 256, 256), 256)]
    wkv[y] = wkvs[y % 2]

    twin = device(z, y, other, x, h)

    def cache_twin(i):
        buf = (kb, vb)[i]
        return remote(buf.at[mine], buf.at[mine], s_kc.at[i], r_kc.at[i], twin)

    for i in range(2):
        local[4 + i].wait()
        copy = cache_twin(i)
        copy.start()
        sends.append(copy)

    for d in range(1, 8):
        hid_y(d).wait_recv()

    def hid_x(d):
        rows = pl.ds(pl.multiple_of(x * 64, 64), 64)
        return remote(hs.at[rows], hs.at[rows], s_hx.at[d], r_hx.at[d], device(z, y, core, lax.rem(x + d, NX), h))

    for d in range(1, NX):
        copy = hid_x(d)
        copy.start()
        sends.append(copy)

    for d in range(1, NY):
        for i in range(2):
            weights(d, i).wait_recv()

    def cache_y(i):
        buf = (kb, vb)[i]
        return remote(buf.at[mine], buf.at[mine], s_ky.at[i], r_ky.at[i], device(z, keys_y, core, x, h))

    for i in range(2):
        copy = cache_y(i)
        copy.start()
        sends.append(copy)

    def out_weights(d):
        to = lax.rem(y + d, NY)
        return remote(
            wos.at[pl.ds(pl.multiple_of(to * 256, 256), 256)], wo.at[y], s_wo.at[d], r_wo.at[d],
            device(z, to, core, x, h),
        )

    local[6].wait()
    for d in range(1, NY):
        copy = out_weights(d)
        copy.start()
        sends.append(copy)
    wo[y] = wos[pl.ds(pl.multiple_of(y * 256, 256), 256), :]

    wqf = wq[...].reshape(512, 256)
    wkvf = wkv[...].reshape(512, 128)

    def project(block):
        rows = pl.ds(pl.multiple_of(block * 64, 64), 64)
        part = hs[rows, :]
        both = dot(part, wqf)
        yp[0, rows, :] = both[:, :128]
        yp[1, rows, :] = both[:, 128:]
        yp[2, rows, :] = dot(part, wkvf)

    project(x)
    for d in range(1, NX):
        hid_x(d).wait_recv()
        project(lax.rem(x + NX - d, NX))

    half = 16 * (y // 2)
    for b in range(NZ):
        kvs[b] = yp[2, pl.ds(pl.multiple_of(32 * b + half + 8 * other, 8), 8), :]
    pair = [
        remote(yp.at[other], yin, s_pc.at[0], r_pc.at[0], twin),
        remote(kvs, kvin, s_pc.at[1], r_pc.at[1], twin),
    ]
    for copy in pair:
        copy.start()
        sends.append(copy)
    for copy in pair:
        copy.wait_recv()
    for b in range(NZ):
        rows = slice(32 * b, 32 * b + 32)
        p2s[b, 0:32, :] = yp[core, rows, :] + yin[rows, :]
        p2s[b, 32:40, :] = yp[2, pl.ds(pl.multiple_of(32 * b + half + 8 * core, 8), 8), :] + kvin[b]

    def zdev(d):
        to = lax.rem(z + d, NZ)
        return to, device(to, y, core, x, h)

    def p2(d):
        to, dev = zdev(d)
        return remote(p2s.at[to], p2d.at[z], s_p2.at[d], r_p2.at[d], dev)

    for d in range(1, NZ):
        copy = p2(d)
        copy.start()
        sends.append(copy)
    p2d[z] = p2s[z]
    for d in range(1, NZ):
        p2(d).wait_recv()
    total = p2d[0]
    for b in range(1, NZ):
        total = total + p2d[b]
    zrows = pl.ds(pl.multiple_of(z * 32, 32), 32)
    qb[0, zrows, :] = total[:32].astype(BF16)

    def zdev2(d, j):
        to = lax.rem(z + d, NZ)
        return to, device(to, (y, heads_y)[j], core, x, h)

    def p3(d, j):
        to, dev = zdev2(d, j)
        return remote(qb.at[0, zrows], qb.at[j, zrows], s_p3.at[j, d], r_p3.at[j, d], dev)

    pairs = [(d, j) for d in (4, 3, 5, 2, 6, 1, 7, 0) for j in (1, 0) if (d, j) != (0, 0)]
    for d, j in pairs:
        copy = p3(d, j)
        copy.start()
        sends.append(copy)

    msgs[mine, 0:8, :] = total[32:]
    msgs[mine, 8:16, :] = jnp.full((8, 128), len_ref[0].astype(F32), F32)

    def message(d, k):
        dev = device(z, lax.rem(y + d, NY), lax.rem(core + k, 2), x, h)
        return remote(msgs.at[mine], msgs.at[mine], s_m.at[k, d], r_m.at[k, d], dev)

    line = [(d, k) for d in range(NY) for k in range(2) if (d, k) != (0, 0)]
    for d, k in line:
        copy = message(d, k)
        copy.start()
        sends.append(copy)
    for d, j in pairs:
        p3(d, j).wait_recv()

    scale = LOG2E / math.sqrt(128.0)
    queries = qb[...].reshape(512, 128)
    m_s[...] = jnp.full((512, 1), NEG, F32)
    l_s[...] = jnp.zeros((512, 1), F32)
    acc[...] = jnp.zeros((512, 128), F32)

    def absorb(rows, scores, values):
        before = m_s[0:rows]
        raised = jnp.maximum(before, jnp.max(scores, axis=1, keepdims=True))
        shrink = jnp.exp2(before - raised)
        weight = jnp.exp2(scores - raised)
        l_s[0:rows] = l_s[0:rows] * shrink + jnp.sum(weight, axis=1, keepdims=True)
        acc[0:rows] = acc[0:rows] * shrink + dot(weight.astype(BF16), values)
        m_s[0:rows] = raised

    def shard(index):
        filled = jnp.concatenate([msgs[index, 8:9, :]] * 4, axis=1)
        place = lax.broadcasted_iota(jnp.int32, (1, 512), 1).astype(F32)
        bias = jnp.where(place < filled, 0.0, NEG)
        absorb(512, dot_t(queries, kb[index]) * scale + bias, vb[index])

    def relay(i):
        index = keys_y * 2 + core
        buf = (kb, vb)[i]
        return remote(buf.at[index], buf.at[index], s_kr.at[i], r_kr.at[i], twin)

    for i in range(2):
        cache_y(i).wait_recv()
        copy = relay(i)
        copy.start()
        sends.append(copy)
    shard(mine)
    for d, k in line:
        message(d, k).wait_recv()
    for i in range(2):
        cache_twin(i).wait_recv()
    shard(y * 2 + other)
    shard(keys_y * 2 + core)

    new_keys = jnp.concatenate([msgs[i, 0:8, :] for i in (0, 1, 4, 5)], axis=0).astype(BF16)
    new_values = jnp.concatenate([msgs[i, 0:8, :] for i in (2, 3, 6, 7)], axis=0).astype(BF16)
    key_at = lax.broadcasted_iota(jnp.int32, (256, 32), 1) + z * 32
    row_at = lax.broadcasted_iota(jnp.int32, (256, 32), 0)
    absorb(256, jnp.where(key_at <= row_at, dot_t(queries[:256], new_keys) * scale, NEG), new_values)

    for i in range(2):
        relay(i).wait_recv()
    shard(keys_y * 2 + other)

    sums = l_s[...]
    shared = (acc[...] / sums).astype(BF16)
    level = m_s[...] + jnp.log2(sums)
    diagonal = lax.broadcasted_iota(jnp.int32, (32, 128), 0) == lax.broadcasted_iota(jnp.int32, (32, 128), 1)
    row16 = lax.broadcasted_iota(jnp.int32, (16, 128), 0)
    for j in range(2):
        for b in range(NZ):
            rows = slice(256 * j + 32 * b, 256 * j + 32 * b + 32)
            po[j, b, 0:32, :] = shared[rows]
            line_of = jnp.sum(jnp.where(diagonal, level[rows], 0.0), axis=0, keepdims=True)
            high = line_of.astype(BF16).astype(F32)
            mid = (line_of - high).astype(BF16).astype(F32)
            low = line_of - high - mid
            po[j, b, 32:48, :] = jnp.where(row16 == 0, high, jnp.where(row16 == 1, mid, low)).astype(BF16)

    def p5(d, j):
        to, dev = zdev2(d, j)
        return remote(po.at[j, to], pod.at[j, z], s_p5.at[j, d], r_p5.at[j, d], dev)

    for d, j in pairs:
        copy = p5(d, j)
        copy.start()
        sends.append(copy)
    pod[0, z] = po[0, z]
    for d, j in pairs:
        p5(d, j).wait_recv()

    levels, parts = [], []
    for j in range(2):
        for b in range(NZ):
            rows = pod[j, b, 32:48, :].astype(F32)
            line_of = rows[0:1] + rows[1:2] + rows[2:3]
            spread = jnp.where(diagonal, jnp.broadcast_to(line_of, (32, 128)), 0.0)
            levels.append(jnp.sum(spread, axis=1, keepdims=True))
            parts.append(pod[j, b, 0:32, :].astype(F32))
    top = functools.reduce(jnp.maximum, levels)
    shares = [jnp.exp2(one - top) for one in levels]
    whole = functools.reduce(jnp.add, shares)
    merged = functools.reduce(jnp.add, [part * share for part, share in zip(parts, shares)])
    att[0, zrows, :] = (merged / whole).astype(BF16)

    def p6(d):
        to, dev = zdev(d)
        return remote(att.at[0, zrows], att.at[0, zrows], s_p6.at[d], r_p6.at[d], dev)

    for d in range(1, NZ):
        copy = p6(d)
        copy.start()
        sends.append(copy)
    for d in range(1, NZ):
        p6(d).wait_recv()
    across = remote(att.at[0], att.at[1], s_rc, r_rc, twin)
    across.start()
    sends.append(across)

    for d in range(1, NY):
        out_weights(d).wait_recv()
    head_rows = pl.ds(pl.multiple_of(core * 128, 128), 128)
    twin_rows = pl.ds(pl.multiple_of(other * 128, 128), 128)
    first = [dot(att[0], wo[b, head_rows, :]) for b in range(NY)]
    across.wait_recv()
    for b in range(NY):
        o2s[b] = (first[b] + dot(att[1], wo[b, twin_rows, :])).astype(BF16)

    def p7_copy(i):
        ty, tx, th = lax.rem(y + i % 4, 4), lax.rem(x + i // 8, 4), lax.rem(h + (i // 4) % 2, 2)
        rows = pl.ds(pl.multiple_of((tx * NH + th) * 32, 32), 32)
        return remote(
            o2s.at[ty, rows], p7.at[tp * NY + y], s_p7.at[i], r_p7.at[i], device(z, ty, core, tx, th)
        )

    def p7_start(i, carry):
        p7_copy(i).start()
        return carry

    def p7_recv(i, carry):
        p7_copy(i).wait_recv()
        return carry

    def p7_send(i, carry):
        p7_copy(i).wait_send()
        return carry

    lax.fori_loop(1, 32, p7_start, 0)
    p7[tp * NY + y] = o2s[y, own_rows, :]
    lax.fori_loop(1, 32, p7_recv, 0)
    result = p7[0].astype(F32)
    for b in range(1, 32):
        result = result + p7[b].astype(F32)
    out_ref[...] = result

    for copy in sends:
        copy.wait_send()
    lax.fori_loop(1, 32, p7_send, 0)


def per_device(hidden_in, w_query, w_key, w_value, w_out, cache_keys, cache_values, prefix_lengths):
    dma = pltpu.SemaphoreType.DMA
    vmem = pltpu.VMEM
    in_hbm = pl.BlockSpec(memory_space=pltpu.HBM)
    return pl.pallas_call(
        kernel,
        out_shape=jax.ShapeDtypeStruct((32, 128), F32),
        in_specs=[in_hbm] * 7 + [pl.BlockSpec(memory_space=pltpu.SMEM)],
        out_specs=pl.BlockSpec(memory_space=pltpu.VMEM),
        scratch_shapes=[
            vmem((256, 512), BF16), vmem((128, 1024), BF16), vmem((2, 128, 128), BF16), vmem((1024, 128), BF16),
            vmem((4, 128, 256), BF16), vmem((4, 128, 128), BF16),
            vmem((4, 256, 128), BF16), vmem((8, 512, 128), BF16), vmem((8, 512, 128), BF16),
            vmem((3, 256, 128), F32), vmem((256, 128), F32), vmem((8, 8, 128), F32), vmem((8, 8, 128), F32),
            vmem((8, 40, 128), F32), vmem((8, 40, 128), F32), vmem((2, 256, 128), BF16), vmem((8, 16, 128), F32),
            vmem((512, 1), F32), vmem((512, 1), F32), vmem((512, 128), F32),
            vmem((2, 8, 48, 128), BF16), vmem((2, 8, 48, 128), BF16),
            vmem((2, 256, 128), BF16), vmem((4, 256, 128), BF16), vmem((32, 32, 128), BF16),
            dma((7,)), dma((8,)), dma((8,)), dma((4,)), dma((4,)), dma((2, 4)), dma((2, 4)), dma((4,)), dma((4,)),
            dma((2,)), dma((2,)), dma((2,)), dma((2,)), dma((2,)), dma((2,)),
            dma((2,)), dma((2,)), dma((8,)), dma((8,)), dma((2, 8)), dma((2, 8)), dma((2, 4)), dma((2, 4)),
            dma((2, 8)), dma((2, 8)), dma((8,)), dma((8,)), dma, dma, dma((32,)), dma((32,)),
        ],
        compiler_params=pltpu.CompilerParams(
            collective_id=0, has_side_effects=True, vmem_limit_bytes=56 * 1024 * 1024
        ),
        cost_estimate=pl.CostEstimate(flops=1_000_000_000, bytes_accessed=2_000_000, transcendentals=1_100_000),
        name="attention_block",
    )(
        hidden_in, w_query, w_key, w_value, w_out,
        cache_keys.reshape(cache_keys.shape[0], 128), cache_values.reshape(cache_values.shape[0], 128),
        prefix_lengths,
    )


def solution(mesh):
    placed = (
        P("tp", "ctx"),
        P("ctx", "tp"),
        P("ctx", "tp"),
        P("ctx", "tp"),
        P("tp", "ctx"),
        P("ctx", "tp", None),
        P("ctx", "tp", None),
        P("ctx"),
    )
    return jax.shard_map(
        per_device, mesh=mesh, in_specs=placed, out_specs=P("tp", "ctx"), check_vma=False
    )
```

time: 95.6 us -> 76.9 us (0.80)
  Pallas kernels: 88 us -> 74.7 us
  local copies, waits for them, and re-layouts: 6.52 us -> 1.32 us
    pallas_call x1, Pallas kernels: 88 us -> 74.7 us  [per_device(): pl.pallas_call(kernel, out_shape=jax.ShapeDtypeStruct((32, 128), F32), in...]
    unnamed x15 -> x1, local copies, waits for them, and re-layouts: 6.52 us -> 1.32 us
where the time goes in v2:
time: 76.9 us; the launch traced here: 76.7 us
  Pallas kernels  74.7 us (97%)
  local copies, waits for them, and re-layouts  1.32 us (2%)
    pallas_call x1, Pallas kernels, per_device(): pl.pallas_call(kernel, out_shape=jax.ShapeDtypeStruct((32, 128), F32), in...  74.7 us

profile of v2, /device:TPU:1, one launch (start us, length us, event | category | flops | bytes accessed | tf_op | source)
XLA Modules:
  0.0 76.7 jit_solution(14285376783815960045)
XLA Ops:
  0.7 74.7 %attention_block.1 = f32[32,128]{1,0:T(8,128)} custom-call(bf16[32,128]{1,0:T(8,128)(2,1)} %hid_ref.1, bf16[128,1024]{1,0:T(8,128)(2,1)} %wq_ref.1, bf16[128,128]{1,0:T(8,128)(2,1)} %wk_ref.1, bf16[128,128]{1,0:T(8,128)(2,1)} %wv_ref.1, bf16[1024,128]{1,0:T(8,128)(2,1)} %wo_ref.1, bf16[512,128]{1,0:T(8,128)(2,1)} %bitcast.2, bf16[512,128]{1,0:T(8,128)(2,1)} %bitcast.3, ...), custom_call_target="tpu_custom_call" | custom-call | flops 1000000000 | bytes 2000000 | tf_op jit(solution)/shard_map/attention_block/pallas_call | solution.py:414
  75.4 1.3 %copy.11 = f32[32,128]{1,0:T(8,128)} copy(f32[32,128]{1,0:T(8,128)} %attention_block.1) | data formatting | bytes 32768

commit v3 on v0

v3 whole, which is shorter than its diff:
```python
import functools
import math

import jax
import jax.numpy as jnp
from jax import lax
from jax.experimental import pallas as pl
from jax.experimental.pallas import tpu as pltpu
from jax.sharding import PartitionSpec as P

MESH = pl.DeviceIdType.MESH
F32 = jnp.float32
BF16 = jnp.bfloat16
NZ, NY, NX, NH = 8, 4, 4, 2
LOG2E = 1.0 / math.log(2.0)
NEG = -1e30
KEYS_WITH = 1
HEADS_WITH = 2
GROUPS = (
    "hidden", "query weights", "kv weights", "cache twin", "cache line", "cache relay", "out weights", "pair",
    "queries", "kv pair", "kv", "heads 0", "heads 1", "messages", "partials 0", "partials 1", "attended", "across",
    "plane",
)


def coords():
    c = lax.axis_index("ctx")
    t = lax.axis_index("tp")
    return c // 8, (c // 2) % 4, c % 2, t // 2, t % 2


def device(z, y, core, x, h):
    return ((z * NY + y) * 2 + core, x * NH + h)


def dot(a, b):
    return jnp.dot(a, b, preferred_element_type=F32)


def dot_t(a, b):
    return lax.dot_general(a, b, (((1,), (1,)), ((), ())), preferred_element_type=F32)


def kernel(
    hid_ref, wq_ref, wk_ref, wv_ref, wo_ref, ck_ref, cv_ref, len_ref, out_ref,
    hs, wqs, wkvs, wos, wq, wkv, wo, kb, vb, yp, yin, yk, kvs, kvin, p2s, p2d, p2k, p2e, qb, msgs,
    po, pod, att, o2s, p7, loc, ssem, rsem, s_hx, r_hx,
):
    z, y, core, x, h = coords()
    other = 1 - core
    yf = h * NY + y
    tp = x * NH + h
    mine = y * 2 + core
    own_rows = pl.ds(pl.multiple_of(tp * 32, 32), 32)
    own_cols = pl.ds(pl.multiple_of(y * 128, 128), 128)
    zrows = pl.ds(pl.multiple_of(z * 32, 32), 32)

    def xor_y(bits):
        if bits == 1:
            return y + 1 - 2 * (y % 2)
        return lax.rem(y + 2, NY)

    keys_y, heads_y = xor_y(KEYS_WITH), xor_y(HEADS_WITH)
    twin = device(z, y, other, x, h)

    def remote(src, dst, ssem, rsem, dev):
        return pltpu.make_async_remote_copy(
            src_ref=src, dst_ref=dst, send_sem=ssem, recv_sem=rsem, device_id=dev, device_id_type=MESH
        )

    sent = []

    def group(name, size):
        index = GROUPS.index(name)

        def put(src, dst, dev):
            remote(src, dst, ssem.at[index], rsem.at[index], dev).start()

        def arrived():
            remote(size, size, ssem.at[index], rsem.at[index], twin).wait_recv()

        sent.append(lambda: remote(size, size, ssem.at[index], rsem.at[index], twin).wait_send())
        return put, arrived

    local = [
        pltpu.make_async_copy(hid_ref, hs.at[own_rows, own_cols], loc.at[0]),
        pltpu.make_async_copy(wq_ref, wqs, loc.at[1]),
        pltpu.make_async_copy(wk_ref, wkvs.at[0], loc.at[2]),
        pltpu.make_async_copy(wv_ref, wkvs.at[1], loc.at[3]),
        pltpu.make_async_copy(ck_ref, kb.at[0], loc.at[4]),
        pltpu.make_async_copy(cv_ref, vb.at[0], loc.at[5]),
        pltpu.make_async_copy(wo_ref, wos, loc.at[6]),
    ]
    for copy in local:
        copy.start()

    barrier = pltpu.get_barrier_semaphore()

    def greet(dev):
        pl.semaphore_signal(barrier, inc=1, device_id=dev, device_id_type=MESH)

    def plane(i):
        return lax.rem(y + i % 4, 4), lax.rem(x + i // 8, 4), lax.rem(h + (i // 4) % 2, 2)

    def greet_plane(i, carry):
        to_y, to_x, to_h = plane(i)
        greet(device(z, to_y, core, to_x, to_h))
        return carry

    lax.fori_loop(1, 32, greet_plane, 0)
    for d in range(1, NZ):
        greet(device(lax.rem(z + d, NZ), y, core, x, h))
        greet(device(lax.rem(z + d, NZ), heads_y, core, x, h))
    for d in range(NY):
        greet(device(z, lax.rem(y + d, NY), other, x, h))
    pl.semaphore_wait(barrier, 31 + 2 * (NZ - 1) + NY)

    own_hidden = hs.at[own_rows, own_cols]
    put, hidden_y_arrived = group("hidden", hs.at[0:224, 0:128])
    local[0].wait()
    for d in (4, 3, 5, 2, 6, 1, 7):
        to = lax.rem(yf + d, 8)
        put(own_hidden, own_hidden, device(z, to % 4, core, x, to // 4))

    put, query_weights_arrived = group("query weights", wq.at[0:3])
    local[1].wait()
    for d in (2, 3, 1):
        to = lax.rem(y + d, NY)
        put(wqs.at[:, pl.ds(pl.multiple_of(to * 256, 256), 256)], wq.at[y], device(z, to, core, x, h))
    wq[y] = wqs[:, pl.ds(pl.multiple_of(y * 256, 256), 256)]

    put, cache_twin_arrived = group("cache twin", kb.at[0:2])
    for i, buf in enumerate((kb, vb)):
        local[4 + i].wait()
        put(buf.at[0], buf.at[1], twin)
    for copy in local[2:4]:
        copy.wait()
    wkv[y] = wkvs[y % 2]

    hidden_y_arrived()

    def hidden_x(d):
        rows = pl.ds(pl.multiple_of(x * 64, 64), 64)
        return remote(hs.at[rows], hs.at[rows], s_hx.at[d], r_hx.at[d], device(z, y, core, lax.rem(x + d, NX), h))

    for d in (2, 1, 3):
        hidden_x(d).start()

    put, kv_weights_arrived = group("kv weights", wkv.at[0:3])
    for d in (2, 3, 1):
        to = lax.rem(y + d, NY)
        put(wkvs.at[to % 2], wkv.at[y], device(z, to, core, x, h))

    query_weights_arrived()
    put, cache_line_arrived = group("cache line", kb.at[0:2])
    for buf in (kb, vb):
        put(buf.at[0], buf.at[2], device(z, keys_y, core, x, h))
    wqf = wq[...].reshape(512, 256)

    def project(block):
        rows = pl.ds(pl.multiple_of(block * 64, 64), 64)
        both = dot(hs[rows, :], wqf)
        yp[0, rows, :] = both[:, :128]
        yp[1, rows, :] = both[:, 128:]

    project(x)
    for d in (1, 3, 2):
        hidden_x(d).wait_recv()
        project(lax.rem(x + NX - d, NX))

    put, pair_arrived = group("pair", yin)
    put(yp.at[other], yin, twin)

    put, out_weights_arrived = group("out weights", wo.at[0:3])
    local[6].wait()
    for d in (2, 3, 1):
        to = lax.rem(y + d, NY)
        put(wos.at[pl.ds(pl.multiple_of(to * 256, 256), 256)], wo.at[y], device(z, to, core, x, h))
    wo[y] = wos[pl.ds(pl.multiple_of(y * 256, 256), 256), :]

    pair_arrived()
    for b in range(NZ):
        rows = slice(32 * b, 32 * b + 32)
        p2s[b] = yp[core, rows, :] + yin[rows, :]

    def zdev(d, at_y=y):
        to = lax.rem(z + d, NZ)
        return to, device(to, at_y, core, x, h)

    put, queries_arrived = group("queries", p2d.at[0:7])
    for d in (4, 3, 5, 2, 6, 1, 7):
        to, dev = zdev(d)
        put(p2s.at[to], p2d.at[z], dev)
    p2d[z] = p2s[z]

    kv_weights_arrived()
    yk[...] = dot(hs[...], wkv[...].reshape(512, 128))
    half = 16 * (y // 2)
    for b in range(NZ):
        kvs[b] = yk[pl.ds(pl.multiple_of(32 * b + half + 8 * other, 8), 8), :]
    put, kv_pair_arrived = group("kv pair", kvs)
    put(kvs, kvin, twin)
    kv_pair_arrived()
    for b in range(NZ):
        p2k[b] = yk[pl.ds(pl.multiple_of(32 * b + half + 8 * core, 8), 8), :] + kvin[b]
    put, kv_arrived = group("kv", p2e.at[0:7])
    for d in (4, 3, 5, 2, 6, 1, 7):
        to, dev = zdev(d)
        put(p2k.at[to], p2e.at[z], dev)
    p2e[z] = p2k[z]

    queries_arrived()
    total = p2d[0]
    for b in range(1, NZ):
        total = total + p2d[b]
    qb[0, zrows, :] = total.astype(BF16)
    put0, heads0_arrived = group("heads 0", qb.at[0, 0:224])
    put1, heads1_arrived = group("heads 1", qb.at[1])
    for d in (4, 3, 5, 2, 6, 1, 7, 0):
        put1(qb.at[0, zrows], qb.at[1, zrows], zdev(d, heads_y)[1])
    for d in (4, 3, 5, 2, 6, 1, 7):
        put0(qb.at[0, zrows], qb.at[0, zrows], zdev(d)[1])

    kv_arrived()
    total = p2e[0]
    for b in range(1, NZ):
        total = total + p2e[b]
    msgs[mine, 0:8, :] = total
    msgs[mine, 8:16, :] = jnp.full((8, 128), len_ref[0].astype(F32), F32)
    put, messages_arrived = group("messages", msgs.at[0:7])
    for d in (2, 3, 1, 0):
        for k in range(2):
            if (d, k) != (0, 0):
                put(msgs.at[mine], msgs.at[mine], device(z, lax.rem(y + d, NY), lax.rem(core + k, 2), x, h))

    cache_line_arrived()
    put, cache_relay_arrived = group("cache relay", kb.at[0:2])
    for buf in (kb, vb):
        put(buf.at[2], buf.at[3], twin)
    cache_twin_arrived()
    messages_arrived()
    cache_relay_arrived()

    scale = LOG2E / math.sqrt(128.0)
    place = lax.broadcasted_iota(jnp.int32, (1, 512), 1).astype(F32)
    bias = []
    for index in (mine, y * 2 + other, keys_y * 2 + core, keys_y * 2 + other):
        filled = jnp.concatenate([msgs[index, 8:9, :]] * 4, axis=1)
        bias.append(jnp.where(place < filled, 0.0, NEG))
    bias = jnp.concatenate(bias, axis=1)
    keys = kb[...].reshape(2048, 128)
    values = vb[...].reshape(2048, 128)
    diagonal = lax.broadcasted_iota(jnp.int32, (32, 128), 0) == lax.broadcasted_iota(jnp.int32, (32, 128), 1)
    row16 = lax.broadcasted_iota(jnp.int32, (16, 128), 0)

    def attend(j, new):
        queries = qb[j]
        scores = dot_t(queries, keys) * scale + bias
        top = jnp.max(scores, axis=1, keepdims=True)
        if new:
            new_keys = jnp.concatenate([msgs[i, 0:8, :] for i in (0, 1, 4, 5)], axis=0).astype(BF16)
            new_values = jnp.concatenate([msgs[i, 0:8, :] for i in (2, 3, 6, 7)], axis=0).astype(BF16)
            key_at = lax.broadcasted_iota(jnp.int32, (256, 32), 1) + z * 32
            row_at = lax.broadcasted_iota(jnp.int32, (256, 32), 0)
            fresh = jnp.where(key_at <= row_at, dot_t(queries, new_keys) * scale, NEG)
            top = jnp.maximum(top, jnp.max(fresh, axis=1, keepdims=True))
        weight = jnp.exp2(scores - top)
        sums = jnp.sum(weight, axis=1, keepdims=True)
        mixed = dot(weight.astype(BF16), values)
        if new:
            weight = jnp.exp2(fresh - top)
            sums = sums + jnp.sum(weight, axis=1, keepdims=True)
            mixed = mixed + dot(weight.astype(BF16), new_values)
        shared = (mixed / sums).astype(BF16)
        level = top + jnp.log2(sums)
        for b in range(NZ):
            rows = slice(32 * b, 32 * b + 32)
            po[j, b, 0:32, :] = shared[rows]
            line = jnp.sum(jnp.where(diagonal, level[rows], 0.0), axis=0, keepdims=True)
            high = line.astype(BF16).astype(F32)
            mid = (line - high).astype(BF16).astype(F32)
            low = line - high - mid
            po[j, b, 32:48, :] = jnp.where(row16 == 0, high, jnp.where(row16 == 1, mid, low)).astype(BF16)

    put0, partials0_arrived = group("partials 0", pod.at[0, 0:7])
    put1, partials1_arrived = group("partials 1", pod.at[1])
    heads1_arrived()
    attend(1, False)
    for d in (4, 3, 5, 2, 6, 1, 7, 0):
        to, dev = zdev(d, heads_y)
        put1(po.at[1, to], pod.at[1, z], dev)
    heads0_arrived()
    attend(0, True)
    for d in (4, 3, 5, 2, 6, 1, 7):
        to, dev = zdev(d)
        put0(po.at[0, to], pod.at[0, z], dev)
    pod[0, z] = po[0, z]
    partials0_arrived()
    partials1_arrived()

    levels, parts = [], []
    for j in range(2):
        for b in range(NZ):
            rows = pod[j, b, 32:48, :].astype(F32)
            line = rows[0:1] + rows[1:2] + rows[2:3]
            spread = jnp.where(diagonal, jnp.broadcast_to(line, (32, 128)), 0.0)
            levels.append(jnp.sum(spread, axis=1, keepdims=True))
            parts.append(pod[j, b, 0:32, :].astype(F32))
    top = functools.reduce(jnp.maximum, levels)
    shares = [jnp.exp2(one - top) for one in levels]
    whole = functools.reduce(jnp.add, shares)
    merged = functools.reduce(jnp.add, [part * share for part, share in zip(parts, shares)])
    att[0, zrows, :] = (merged / whole).astype(BF16)

    put, attended_arrived = group("attended", att.at[0, 0:224])
    for d in (4, 3, 5, 2, 6, 1, 7):
        put(att.at[0, zrows], att.at[0, zrows], zdev(d)[1])
    out_weights_arrived()
    attended_arrived()
    put, across_arrived = group("across", att.at[1])
    put(att.at[0], att.at[1], twin)

    head_rows = pl.ds(pl.multiple_of(core * 128, 128), 128)
    twin_rows = pl.ds(pl.multiple_of(other * 128, 128), 128)
    columns = [lax.rem(y + d, NY) for d in range(NY)]
    first = [dot(att[0], wo[b, head_rows, :]) for b in columns]
    across_arrived()
    put, plane_arrived = group("plane", p7.at[0:31])
    for d in range(NY):
        to_y = columns[d]
        o2s[to_y] = (first[d] + dot(att[1], wo[to_y, twin_rows, :])).astype(BF16)
        for dh in (1, 0):
            for dx in (2, 1, 3, 0):
                if (d, dh, dx) == (0, 0, 0):
                    continue
                to_x, to_h = lax.rem(x + dx, NX), lax.rem(h + dh, NH)
                rows = pl.ds(pl.multiple_of((to_x * NH + to_h) * 32, 32), 32)
                put(o2s.at[to_y, rows], p7.at[tp * NY + y], device(z, to_y, core, to_x, to_h))
    p7[tp * NY + y] = o2s[y, own_rows, :]
    for d in range(1, NX):
        hidden_x(d).wait_send()
    for wait in sent[:-1]:
        wait()
    plane_arrived()
    result = p7[0].astype(F32)
    for b in range(1, 32):
        result = result + p7[b].astype(F32)
    out_ref[...] = result
    sent[-1]()


def per_device(hidden_in, w_query, w_key, w_value, w_out, cache_keys, cache_values, prefix_lengths):
    dma = pltpu.SemaphoreType.DMA
    vmem = pltpu.VMEM
    in_hbm = pl.BlockSpec(memory_space=pltpu.HBM)
    return pl.pallas_call(
        kernel,
        out_shape=jax.ShapeDtypeStruct((32, 128), F32),
        in_specs=[in_hbm] * 7 + [pl.BlockSpec(memory_space=pltpu.SMEM)],
        out_specs=pl.BlockSpec(memory_space=pltpu.VMEM),
        scratch_shapes=[
            vmem((256, 512), BF16), vmem((128, 1024), BF16), vmem((2, 128, 128), BF16), vmem((1024, 128), BF16),
            vmem((4, 128, 256), BF16), vmem((4, 128, 128), BF16), vmem((4, 256, 128), BF16),
            vmem((4, 512, 128), BF16), vmem((4, 512, 128), BF16),
            vmem((2, 256, 128), F32), vmem((256, 128), F32), vmem((256, 128), F32),
            vmem((8, 8, 128), F32), vmem((8, 8, 128), F32),
            vmem((8, 32, 128), F32), vmem((8, 32, 128), F32), vmem((8, 8, 128), F32), vmem((8, 8, 128), F32),
            vmem((2, 256, 128), BF16), vmem((8, 16, 128), F32),
            vmem((2, 8, 48, 128), BF16), vmem((2, 8, 48, 128), BF16),
            vmem((2, 256, 128), BF16), vmem((4, 256, 128), BF16), vmem((32, 32, 128), BF16),
            dma((7,)), dma((len(GROUPS),)), dma((len(GROUPS),)), dma((4,)), dma((4,)),
        ],
        compiler_params=pltpu.CompilerParams(
            collective_id=0, has_side_effects=True, vmem_limit_bytes=56 * 1024 * 1024
        ),
        cost_estimate=pl.CostEstimate(flops=1_000_000_000, bytes_accessed=2_000_000, transcendentals=1_100_000),
        name="attention_block",
    )(
        hidden_in, w_query, w_key, w_value, w_out,
        cache_keys.reshape(cache_keys.shape[0], 128), cache_values.reshape(cache_values.shape[0], 128),
        prefix_lengths,
    )


def solution(mesh):
    placed = (
        P("tp", "ctx"),
        P("ctx", "tp"),
        P("ctx", "tp"),
        P("ctx", "tp"),
        P("tp", "ctx"),
        P("ctx", "tp", None),
        P("ctx", "tp", None),
        P("ctx"),
    )
    return jax.shard_map(
        per_device, mesh=mesh, in_specs=placed, out_specs=P("tp", "ctx"), check_vma=False
    )
```

time: 665 us -> 68.2 us (0.10)
  blocking collectives: 484 us -> 0 us
  waiting for transfers between devices: 129 us -> 0 us
  Pallas kernels: 0 us -> 66 us
  starting transfers between devices: 14.8 us -> 0 us
  between operations: 15 us -> 0.66 us
  matrix products: 10.7 us -> 0 us
    unnamed x1 -> x0, blocking collectives: 284 us -> none
    all_gather x3 -> x0, blocking collectives: 200 us -> none  [the longest x1 81.8 us: per_device(): query_piece = lax.all_gather(queries, 'ctx', axis=0, tiled=True)]
    reduce_scatter x1 -> x0, waiting for transfers between devices: 84.6 us -> none  [per_device(): return lax.psum_scatter(head_terms, 'tp', scatter_dimension=0, tiled=True)]
    pallas_call x0 -> x1, Pallas kernels: none -> 66 us  [per_device(): pl.pallas_call(kernel, out_shape=jax.ShapeDtypeStruct((32, 128), F32), in...]
    all_to_all x3 -> x0, waiting for transfers between devices: 44.6 us -> none  [the longest x1 27.8 us: per_device(): lax.all_to_all(weighted, 'ctx', split_axis=0, concat_axis=0, tiled=True)]
    all_to_all x3 -> x0, starting transfers between devices: 14.8 us -> none  [the longest x1 5.85 us: per_device(): lax.all_to_all(totals, 'ctx', split_axis=0, concat_axis=0, tiled=True)]
    dot_general x6 -> x0, matrix products: 10.7 us -> none  [the longest x2 5.05 us: absorb(): jnp.einsum('rgd,kd->rgk', queries, key_rows, preferred_element_type=jnp.f...]
  transfers between devices with their start and end apart: 4 -> 0, of which waited for: 4 -> 0; matrix products, arithmetic and copies ran while one was open for 1% -> 0% of each run, Pallas kernels for 0% -> 0%
where the time goes in v3:
time: 68.2 us; the launch traced here: 68 us
  Pallas kernels  66 us (97%)
  local copies, waits for them, and re-layouts  1.32 us (2%)
    pallas_call x1, Pallas kernels, per_device(): pl.pallas_call(kernel, out_shape=jax.ShapeDtypeStruct((32, 128), F32), in...  66 us

profile of v3, /device:TPU:1, one launch (start us, length us, event | category | flops | bytes accessed | tf_op | source)
XLA Modules:
  0.0 68.0 jit_solution(5448803373387132750)
XLA Ops:
  0.7 66.0 %attention_block.1 = f32[32,128]{1,0:T(8,128)} custom-call(bf16[32,128]{1,0:T(8,128)(2,1)} %hid_ref.1, bf16[128,1024]{1,0:T(8,128)(2,1)} %wq_ref.1, bf16[128,128]{1,0:T(8,128)(2,1)} %wk_ref.1, bf16[128,128]{1,0:T(8,128)(2,1)} %wv_ref.1, bf16[1024,128]{1,0:T(8,128)(2,1)} %wo_ref.1, bf16[512,128]{1,0:T(8,128)(2,1)} %bitcast.2, bf16[512,128]{1,0:T(8,128)(2,1)} %bitcast.3, ...), custom_call_target="tpu_custom_call" | custom-call | flops 1000000000 | bytes 2000000 | tf_op jit(solution)/shard_map/attention_block/pallas_call | solution.py:356
  66.7 1.3 %copy.11 = f32[32,128]{1,0:T(8,128)} copy(f32[32,128]{1,0:T(8,128)} %attention_block.1) | data formatting | bytes 32768

commit v4 on v3

--- a/solution.py
+++ b/solution.py
@@ -44,7 +44,7 @@
 def kernel(
     hid_ref, wq_ref, wk_ref, wv_ref, wo_ref, ck_ref, cv_ref, len_ref, out_ref,
     hs, wqs, wkvs, wos, wq, wkv, wo, kb, vb, yp, yin, yk, kvs, kvin, p2s, p2d, p2k, p2e, qb, msgs,
-    po, pod, att, o2s, p7, loc, ssem, rsem, s_hx, r_hx,
+    po, pod, att, o2s, p7, loc, ssem, rsem, s_hx, r_hx, known,
 ):
     z, y, core, x, h = coords()
     other = 1 - core
@@ -96,31 +96,31 @@
 
     barrier = pltpu.get_barrier_semaphore()
 
-    def greet(dev):
+    def zdev(d, at_y=y):
+        to = lax.rem(z + d, NZ)
+        return to, device(to, at_y, core, x, h)
+
+    def yring(d):
+        to = lax.rem(yf + d, 8)
+        return device(z, to % 4, core, x, to // 4)
+
+    near = [yring(d) for d in (4, 3, 5, 2, 6, 1, 7)]
+    near += [device(z, y, core, lax.rem(x + d, NX), h) for d in (2, 1, 3)]
+    near += [zdev(1)[1], zdev(7)[1], twin]
+    for dev in near:
         pl.semaphore_signal(barrier, inc=1, device_id=dev, device_id_type=MESH)
-
-    def plane(i):
-        return lax.rem(y + i % 4, 4), lax.rem(x + i // 8, 4), lax.rem(h + (i // 4) % 2, 2)
-
-    def greet_plane(i, carry):
-        to_y, to_x, to_h = plane(i)
-        greet(device(z, to_y, core, to_x, to_h))
-        return carry
-
-    lax.fori_loop(1, 32, greet_plane, 0)
-    for d in range(1, NZ):
-        greet(device(lax.rem(z + d, NZ), y, core, x, h))
-        greet(device(lax.rem(z + d, NZ), heads_y, core, x, h))
-    for d in range(NY):
-        greet(device(z, lax.rem(y + d, NY), other, x, h))
-    pl.semaphore_wait(barrier, 31 + 2 * (NZ - 1) + NY)
+    pl.semaphore_wait(barrier, len(near))
+
+    def tell(i, d):
+        pl.semaphore_signal(known.at[i], inc=1, device_id=zdev(d)[1], device_id_type=MESH)
 
     own_hidden = hs.at[own_rows, own_cols]
     put, hidden_y_arrived = group("hidden", hs.at[0:224, 0:128])
     local[0].wait()
     for d in (4, 3, 5, 2, 6, 1, 7):
-        to = lax.rem(yf + d, 8)
-        put(own_hidden, own_hidden, device(z, to % 4, core, x, to // 4))
+        put(own_hidden, own_hidden, yring(d))
+    tell(0, 1)
+    tell(1, 7)
 
     put, query_weights_arrived = group("query weights", wq.at[0:3])
     local[1].wait()
@@ -137,6 +137,11 @@
         copy.wait()
     wkv[y] = wkvs[y % 2]
 
+    for i in range(2):
+        pl.semaphore_wait(known.at[i], 1)
+    tell(2, 1)
+    tell(3, 7)
+    tell(4, 2)
     hidden_y_arrived()
 
     def hidden_x(d):
@@ -183,10 +188,8 @@
         rows = slice(32 * b, 32 * b + 32)
         p2s[b] = yp[core, rows, :] + yin[rows, :]
 
-    def zdev(d, at_y=y):
-        to = lax.rem(z + d, NZ)
-        return to, device(to, at_y, core, x, h)
-
+    for i in range(2, 5):
+        pl.semaphore_wait(known.at[i], 1)
     put, queries_arrived = group("queries", p2d.at[0:7])
     for d in (4, 3, 5, 2, 6, 1, 7):
         to, dev = zdev(d)
@@ -369,6 +372,7 @@
             vmem((2, 8, 48, 128), BF16), vmem((2, 8, 48, 128), BF16),
             vmem((2, 256, 128), BF16), vmem((4, 256, 128), BF16), vmem((32, 32, 128), BF16),
             dma((7,)), dma((len(GROUPS),)), dma((len(GROUPS),)), dma((4,)), dma((4,)),
+            pltpu.SemaphoreType.REGULAR((5,)),
         ],
         compiler_params=pltpu.CompilerParams(
             collective_id=0, has_side_effects=True, vmem_limit_bytes=56 * 1024 * 1024

time: 68.2 us -> 66 us (0.968)
  Pallas kernels: 66 us -> 63.8 us
    pallas_call x1, Pallas kernels: 66 us -> 63.8 us  [per_device(): pl.pallas_call(kernel, out_shape=jax.ShapeDtypeStruct((32, 128), F32), in...]
where the time goes in v4:
time: 66 us; the launch traced here: 65.8 us
  Pallas kernels  63.8 us (97%)
  local copies, waits for them, and re-layouts  1.32 us (2%)
  between operations  0.66 us (1%)
    pallas_call x1, Pallas kernels, per_device(): pl.pallas_call(kernel, out_shape=jax.ShapeDtypeStruct((32, 128), F32), in...  63.8 us
    unnamed x1, local copies, waits for them, and re-layouts  1.32 us

profile of v4, /device:TPU:1, one launch (start us, length us, event | category | flops | bytes accessed | tf_op | source)
XLA Modules:
  0.0 65.8 jit_solution(12870428849200882944)
XLA Ops:
  0.7 63.8 %attention_block.1 = f32[32,128]{1,0:T(8,128)} custom-call(bf16[32,128]{1,0:T(8,128)(2,1)} %hid_ref.1, bf16[128,1024]{1,0:T(8,128)(2,1)} %wq_ref.1, bf16[128,128]{1,0:T(8,128)(2,1)} %wk_ref.1, bf16[128,128]{1,0:T(8,128)(2,1)} %wv_ref.1, bf16[1024,128]{1,0:T(8,128)(2,1)} %wo_ref.1, bf16[512,128]{1,0:T(8,128)(2,1)} %bitcast.2, bf16[512,128]{1,0:T(8,128)(2,1)} %bitcast.3, ...), custom_call_target="tpu_custom_call" | custom-call | flops 1000000000 | bytes 2000000 | tf_op jit(solution)/shard_map/attention_block/pallas_call | solution.py:359
  64.5 1.3 %copy.11 = f32[32,128]{1,0:T(8,128)} copy(f32[32,128]{1,0:T(8,128)} %attention_block.1) | data formatting | bytes 32768

commit v5 on v4

--- a/solution.py
+++ b/solution.py
@@ -17,7 +17,7 @@
 KEYS_WITH = 1
 HEADS_WITH = 2
 GROUPS = (
-    "hidden", "query weights", "kv weights", "cache twin", "cache line", "cache relay", "out weights", "pair",
+    "query weights", "kv weights", "cache twin", "cache line", "cache relay", "out weights", "pair",
     "queries", "kv pair", "kv", "heads 0", "heads 1", "messages", "partials 0", "partials 1", "attended", "across",
     "plane",
 )
@@ -44,13 +44,12 @@
 def kernel(
     hid_ref, wq_ref, wk_ref, wv_ref, wo_ref, ck_ref, cv_ref, len_ref, out_ref,
     hs, wqs, wkvs, wos, wq, wkv, wo, kb, vb, yp, yin, yk, kvs, kvin, p2s, p2d, p2k, p2e, qb, msgs,
-    po, pod, att, o2s, p7, loc, ssem, rsem, s_hx, r_hx, known,
+    po, pod, att, o2s, p7, loc, ssem, rsem, s_hy, r_hy, s_hx, r_hx, known,
 ):
     z, y, core, x, h = coords()
     other = 1 - core
     yf = h * NY + y
     tp = x * NH + h
-    mine = y * 2 + core
     own_rows = pl.ds(pl.multiple_of(tp * 32, 32), 32)
     own_cols = pl.ds(pl.multiple_of(y * 128, 128), 128)
     zrows = pl.ds(pl.multiple_of(z * 32, 32), 32)
@@ -114,11 +113,26 @@
     def tell(i, d):
         pl.semaphore_signal(known.at[i], inc=1, device_id=zdev(d)[1], device_id_type=MESH)
 
-    own_hidden = hs.at[own_rows, own_cols]
-    put, hidden_y_arrived = group("hidden", hs.at[0:224, 0:128])
+    def block(d):
+        at = lax.rem(yf + 8 - d, 8)
+        rows = pl.ds(pl.multiple_of((x * NH + at // 4) * 32, 32), 32)
+        return hs.at[rows, pl.ds(pl.multiple_of((at % 4) * 128, 128), 128)]
+
+    def hidden_y(d):
+        return remote(block(0), block(0), s_hy.at[d], r_hy.at[d], yring(d))
+
+    def hidden_x(d, view):
+        return remote(view, view, s_hx.at[d], r_hx.at[d], device(z, y, core, lax.rem(x + d, NX), h))
+
+    def forward(d):
+        for dx in (2, 1, 3):
+            hidden_x(dx, block(d)).start()
+
+    x_rows = hs.at[pl.ds(pl.multiple_of(x * 64, 64), 64)]
     local[0].wait()
     for d in (4, 3, 5, 2, 6, 1, 7):
-        put(own_hidden, own_hidden, yring(d))
+        hidden_y(d).start()
+    forward(0)
     tell(0, 1)
     tell(1, 7)
 
@@ -137,19 +151,17 @@
         copy.wait()
     wkv[y] = wkvs[y % 2]
 
+    for d in (1, 7, 2, 6):
+        hidden_y(d).wait_recv()
+        forward(d)
     for i in range(2):
         pl.semaphore_wait(known.at[i], 1)
     tell(2, 1)
     tell(3, 7)
     tell(4, 2)
-    hidden_y_arrived()
-
-    def hidden_x(d):
-        rows = pl.ds(pl.multiple_of(x * 64, 64), 64)
-        return remote(hs.at[rows], hs.at[rows], s_hx.at[d], r_hx.at[d], device(z, y, core, lax.rem(x + d, NX), h))
-
-    for d in (2, 1, 3):
-        hidden_x(d).start()
+    for d in (3, 5, 4):
+        hidden_y(d).wait_recv()
+        forward(d)
 
     put, kv_weights_arrived = group("kv weights", wkv.at[0:3])
     for d in (2, 3, 1):
@@ -170,18 +182,22 @@
 
     project(x)
     for d in (1, 3, 2):
-        hidden_x(d).wait_recv()
+        hidden_x(d, x_rows).wait_recv()
         project(lax.rem(x + NX - d, NX))
 
     put, pair_arrived = group("pair", yin)
     put(yp.at[other], yin, twin)
 
-    put, out_weights_arrived = group("out weights", wo.at[0:3])
+    put, out_weights_arrived = group("out weights", wo.at[0])
     local[6].wait()
-    for d in (2, 3, 1):
-        to = lax.rem(y + d, NY)
-        put(wos.at[pl.ds(pl.multiple_of(to * 256, 256), 256)], wo.at[y], device(z, to, core, x, h))
-    wo[y] = wos[pl.ds(pl.multiple_of(y * 256, 256), 256), :]
+    for pair_core in range(2):
+        for chip in range(2):
+            def rows_of(at):
+                return pl.ds(pl.multiple_of((at // 2) * 512 + 256 * chip + 128 * pair_core, 128), 128)
+
+            there = wo.at[pair_core, pl.ds(128 * chip, 128)]
+            put(wos.at[rows_of(heads_y)], there.at[:, pl.ds(128, 128)], device(z, heads_y, core, x, h))
+            wo[pair_core, 128 * chip : 128 * chip + 128, 0:128] = wos[rows_of(y), :]
 
     pair_arrived()
     for b in range(NZ):
@@ -200,12 +216,7 @@
     yk[...] = dot(hs[...], wkv[...].reshape(512, 128))
     half = 16 * (y // 2)
     for b in range(NZ):
-        kvs[b] = yk[pl.ds(pl.multiple_of(32 * b + half + 8 * other, 8), 8), :]
-    put, kv_pair_arrived = group("kv pair", kvs)
-    put(kvs, kvin, twin)
-    kv_pair_arrived()
-    for b in range(NZ):
-        p2k[b] = yk[pl.ds(pl.multiple_of(32 * b + half + 8 * core, 8), 8), :] + kvin[b]
+        p2k[b] = yk[pl.ds(pl.multiple_of(32 * b + half, 16), 16), :]
     put, kv_arrived = group("kv", p2e.at[0:7])
     for d in (4, 3, 5, 2, 6, 1, 7):
         to, dev = zdev(d)
@@ -228,13 +239,18 @@
     total = p2e[0]
     for b in range(1, NZ):
         total = total + p2e[b]
-    msgs[mine, 0:8, :] = total
-    msgs[mine, 8:16, :] = jnp.full((8, 128), len_ref[0].astype(F32), F32)
-    put, messages_arrived = group("messages", msgs.at[0:7])
-    for d in (2, 3, 1, 0):
-        for k in range(2):
-            if (d, k) != (0, 0):
-                put(msgs.at[mine], msgs.at[mine], device(z, lax.rem(y + d, NY), lax.rem(core + k, 2), x, h))
+    fill = jnp.full((8, 128), len_ref[0].astype(F32), F32)
+    kvs[0:16, :] = total
+    kvs[16:24, :] = fill
+    put, kv_pair_arrived = group("kv pair", kvs)
+    put(kvs, kvin, twin)
+    kv_pair_arrived()
+    row8 = lax.broadcasted_iota(jnp.int32, (8, 128), 0)
+    msgs[y, 0:16, :] = total + kvin[0:16, :]
+    msgs[y, 16:24, :] = jnp.where(row8 == core, fill, kvin[16:24, :])
+    put, messages_arrived = group("messages", msgs.at[0:3])
+    for d in (2, 3, 1):
+        put(msgs.at[y], msgs.at[y], device(z, lax.rem(y + d, NY), core, x, h))
 
     cache_line_arrived()
     put, cache_relay_arrived = group("cache relay", kb.at[0:2])
@@ -246,9 +262,12 @@
 
     scale = LOG2E / math.sqrt(128.0)
     place = lax.broadcasted_iota(jnp.int32, (1, 512), 1).astype(F32)
-    bias = []
-    for index in (mine, y * 2 + other, keys_y * 2 + core, keys_y * 2 + other):
-        filled = jnp.concatenate([msgs[index, 8:9, :]] * 4, axis=1)
+    bias, lengths = [], []
+    for chip in (y, keys_y):
+        pair = (msgs[chip, 16:17, :], msgs[chip, 17:18, :])
+        lengths += [jnp.where(core == 0, *pair), jnp.where(core == 0, *pair[::-1])]
+    for length in lengths:
+        filled = jnp.concatenate([length] * 4, axis=1)
         bias.append(jnp.where(place < filled, 0.0, NEG))
     bias = jnp.concatenate(bias, axis=1)
     keys = kb[...].reshape(2048, 128)
@@ -261,8 +280,8 @@
         scores = dot_t(queries, keys) * scale + bias
         top = jnp.max(scores, axis=1, keepdims=True)
         if new:
-            new_keys = jnp.concatenate([msgs[i, 0:8, :] for i in (0, 1, 4, 5)], axis=0).astype(BF16)
-            new_values = jnp.concatenate([msgs[i, 0:8, :] for i in (2, 3, 6, 7)], axis=0).astype(BF16)
+            new_keys = jnp.concatenate([msgs[i, 0:16, :] for i in (0, 2)], axis=0).astype(BF16)
+            new_values = jnp.concatenate([msgs[i, 0:16, :] for i in (1, 3)], axis=0).astype(BF16)
             key_at = lax.broadcasted_iota(jnp.int32, (256, 32), 1) + z * 32
             row_at = lax.broadcasted_iota(jnp.int32, (256, 32), 0)
             fresh = jnp.where(key_at <= row_at, dot_t(queries, new_keys) * scale, NEG)
@@ -313,40 +332,43 @@
     shares = [jnp.exp2(one - top) for one in levels]
     whole = functools.reduce(jnp.add, shares)
     merged = functools.reduce(jnp.add, [part * share for part, share in zip(parts, shares)])
-    att[0, zrows, :] = (merged / whole).astype(BF16)
-
-    put, attended_arrived = group("attended", att.at[0, 0:224])
-    for d in (4, 3, 5, 2, 6, 1, 7):
-        put(att.at[0, zrows], att.at[0, zrows], zdev(d)[1])
+
+    own_lanes = pl.ds(pl.multiple_of((y % 2) * 128, 128), 128)
+    att[0, zrows, own_lanes] = (merged / whole).astype(BF16)
+    put, attended_arrived = group("attended", att.at[0, 0:240])
+    attended = att.at[0, zrows, own_lanes]
+    for d in (4, 3, 5, 2, 6, 1, 7, 0):
+        put(attended, attended, zdev(d, keys_y)[1])
+    for d in (4, 3, 5, 2, 6, 1, 7):
+        put(attended, attended, zdev(d)[1])
     out_weights_arrived()
     attended_arrived()
     put, across_arrived = group("across", att.at[1])
     put(att.at[0], att.at[1], twin)
 
-    head_rows = pl.ds(pl.multiple_of(core * 128, 128), 128)
-    twin_rows = pl.ds(pl.multiple_of(other * 128, 128), 128)
-    columns = [lax.rem(y + d, NY) for d in range(NY)]
-    first = [dot(att[0], wo[b, head_rows, :]) for b in columns]
+    first = dot(att[0], wo[core])
     across_arrived()
-    put, plane_arrived = group("plane", p7.at[0:31])
-    for d in range(NY):
-        to_y = columns[d]
-        o2s[to_y] = (first[d] + dot(att[1], wo[to_y, twin_rows, :])).astype(BF16)
-        for dh in (1, 0):
-            for dx in (2, 1, 3, 0):
-                if (d, dh, dx) == (0, 0, 0):
-                    continue
-                to_x, to_h = lax.rem(x + dx, NX), lax.rem(h + dh, NH)
-                rows = pl.ds(pl.multiple_of((to_x * NH + to_h) * 32, 32), 32)
-                put(o2s.at[to_y, rows], p7.at[tp * NY + y], device(z, to_y, core, to_x, to_h))
-    p7[tp * NY + y] = o2s[y, own_rows, :]
+    put, plane_arrived = group("plane", p7.at[0:15])
+    both = (first + dot(att[1], wo[other])).astype(BF16)
+    o2s[0] = both[:, :128]
+    o2s[1] = both[:, 128:]
+    for e, dh in ((0, 1), (1, 1), (1, 0), (0, 0)):
+        for dx in (2, 1, 3, 0):
+            if (e, dh, dx) == (0, 0, 0):
+                continue
+            to_x, to_h = lax.rem(x + dx, NX), lax.rem(h + dh, NH)
+            rows = pl.ds(pl.multiple_of((to_x * NH + to_h) * 32, 32), 32)
+            put(o2s.at[e, rows], p7.at[2 * tp + e], device(z, (y, heads_y)[e], core, to_x, to_h))
+    p7[2 * tp] = o2s[0, own_rows, :]
+    for d in range(1, 8):
+        hidden_y(d).wait_send()
     for d in range(1, NX):
-        hidden_x(d).wait_send()
+        hidden_x(d, x_rows).wait_send()
     for wait in sent[:-1]:
         wait()
     plane_arrived()
     result = p7[0].astype(F32)
-    for b in range(1, 32):
+    for b in range(1, 16):
         result = result + p7[b].astype(F32)
     out_ref[...] = result
     sent[-1]()
@@ -363,15 +385,15 @@
         out_specs=pl.BlockSpec(memory_space=pltpu.VMEM),
         scratch_shapes=[
             vmem((256, 512), BF16), vmem((128, 1024), BF16), vmem((2, 128, 128), BF16), vmem((1024, 128), BF16),
-            vmem((4, 128, 256), BF16), vmem((4, 128, 128), BF16), vmem((4, 256, 128), BF16),
+            vmem((4, 128, 256), BF16), vmem((4, 128, 128), BF16), vmem((2, 256, 256), BF16),
             vmem((4, 512, 128), BF16), vmem((4, 512, 128), BF16),
             vmem((2, 256, 128), F32), vmem((256, 128), F32), vmem((256, 128), F32),
-            vmem((8, 8, 128), F32), vmem((8, 8, 128), F32),
-            vmem((8, 32, 128), F32), vmem((8, 32, 128), F32), vmem((8, 8, 128), F32), vmem((8, 8, 128), F32),
-            vmem((2, 256, 128), BF16), vmem((8, 16, 128), F32),
+            vmem((24, 128), F32), vmem((24, 128), F32),
+            vmem((8, 32, 128), F32), vmem((8, 32, 128), F32), vmem((8, 16, 128), F32), vmem((8, 16, 128), F32),
+            vmem((2, 256, 128), BF16), vmem((4, 24, 128), F32),
             vmem((2, 8, 48, 128), BF16), vmem((2, 8, 48, 128), BF16),
-            vmem((2, 256, 128), BF16), vmem((4, 256, 128), BF16), vmem((32, 32, 128), BF16),
-            dma((7,)), dma((len(GROUPS),)), dma((len(GROUPS),)), dma((4,)), dma((4,)),
+            vmem((2, 256, 256), BF16), vmem((2, 256, 128), BF16), vmem((16, 32, 128), BF16),
+            dma((7,)), dma((len(GROUPS),)), dma((len(GROUPS),)), dma((8,)), dma((8,)), dma((4,)), dma((4,)),
             pltpu.SemaphoreType.REGULAR((5,)),
         ],
         compiler_params=pltpu.CompilerParams(

time: 66 us -> 62.6 us (0.948)
  Pallas kernels: 63.8 us -> 60.4 us
    pallas_call x1, Pallas kernels: 63.8 us -> 60.4 us  [per_device(): pl.pallas_call(kernel, out_shape=jax.ShapeDtypeStruct((32, 128), F32), in...]
where the time goes in v5:
time: 62.6 us; the launch traced here: 62.4 us
  Pallas kernels  60.4 us (96%)
  local copies, waits for them, and re-layouts  1.32 us (2%)
  between operations  0.66 us (1%)
    pallas_call x1, Pallas kernels, per_device(): pl.pallas_call(kernel, out_shape=jax.ShapeDtypeStruct((32, 128), F32), in...  60.4 us
    unnamed x1, local copies, waits for them, and re-layouts  1.32 us

profile of v5, /device:TPU:1, one launch (start us, length us, event | category | flops | bytes accessed | tf_op | source)
XLA Modules:
  0.0 62.4 jit_solution(14443777457356925635)
XLA Ops:
  0.7 60.4 %attention_block.1 = f32[32,128]{1,0:T(8,128)} custom-call(bf16[32,128]{1,0:T(8,128)(2,1)} %hid_ref.1, bf16[128,1024]{1,0:T(8,128)(2,1)} %wq_ref.1, bf16[128,128]{1,0:T(8,128)(2,1)} %wk_ref.1, bf16[128,128]{1,0:T(8,128)(2,1)} %wv_ref.1, bf16[1024,128]{1,0:T(8,128)(2,1)} %wo_ref.1, bf16[512,128]{1,0:T(8,128)(2,1)} %bitcast.2, bf16[512,128]{1,0:T(8,128)(2,1)} %bitcast.3, ...), custom_call_target="tpu_custom_call" | custom-call | flops 1000000000 | bytes 2000000 | tf_op jit(solution)/shard_map/attention_block/pallas_call | solution.py:381
  61.1 1.3 %copy.11 = f32[32,128]{1,0:T(8,128)} copy(f32[32,128]{1,0:T(8,128)} %attention_block.1) | data formatting | bytes 32768

commit v6 on v5

--- a/solution.py
+++ b/solution.py
@@ -17,8 +17,9 @@
 KEYS_WITH = 1
 HEADS_WITH = 2
 GROUPS = (
-    "query weights", "kv weights", "cache twin", "cache line", "cache relay", "out weights", "pair",
-    "queries", "kv pair", "kv", "heads 0", "heads 1", "messages", "partials 0", "partials 1", "attended", "across",
+    "query weights", "kv weights", "cache twin", "cache line", "cache relay", "length twin", "length line",
+    "length relay", "out weights", "pair",
+    "queries", "kv pair", "kv", "heads 0", "heads 1", "messages", "partials 0", "partials 1", "levels 0", "levels 1", "attended", "across",
     "plane",
 )
 
@@ -43,8 +44,8 @@
 
 def kernel(
     hid_ref, wq_ref, wk_ref, wv_ref, wo_ref, ck_ref, cv_ref, len_ref, out_ref,
-    hs, wqs, wkvs, wos, wq, wkv, wo, kb, vb, yp, yin, yk, kvs, kvin, p2s, p2d, p2k, p2e, qb, msgs,
-    po, pod, att, o2s, p7, loc, ssem, rsem, s_hy, r_hy, s_hx, r_hx, known,
+    hs, wqs, wkvs, wos, wq, wkv, wo, kb, vb, yp, yin, yk, kvs, kvin, fill, p2s, p2d, p2k, p2e, qb, msgs,
+    po, pod, pl_s, pl_d, att, o2s, p7, loc, ssem, rsem, s_hy, r_hy, s_hx, r_hx, known,
 ):
     z, y, core, x, h = coords()
     other = 1 - core
@@ -143,6 +144,9 @@
         put(wqs.at[:, pl.ds(pl.multiple_of(to * 256, 256), 256)], wq.at[y], device(z, to, core, x, h))
     wq[y] = wqs[:, pl.ds(pl.multiple_of(y * 256, 256), 256)]
 
+    fill[0:1, :] = jnp.full((1, 128), len_ref[0].astype(F32), F32)
+    put, length_twin_arrived = group("length twin", fill.at[0:1])
+    put(fill.at[0:1], fill.at[1:2], twin)
     put, cache_twin_arrived = group("cache twin", kb.at[0:2])
     for i, buf in enumerate((kb, vb)):
         local[4 + i].wait()
@@ -169,6 +173,8 @@
         put(wkvs.at[to % 2], wkv.at[y], device(z, to, core, x, h))
 
     query_weights_arrived()
+    put, length_line_arrived = group("length line", fill.at[0:1])
+    put(fill.at[0:1], fill.at[2:3], device(z, keys_y, core, x, h))
     put, cache_line_arrived = group("cache line", kb.at[0:2])
     for buf in (kb, vb):
         put(buf.at[0], buf.at[2], device(z, keys_y, core, x, h))
@@ -239,95 +245,93 @@
     total = p2e[0]
     for b in range(1, NZ):
         total = total + p2e[b]
-    fill = jnp.full((8, 128), len_ref[0].astype(F32), F32)
-    kvs[0:16, :] = total
-    kvs[16:24, :] = fill
+    kvs[...] = total
     put, kv_pair_arrived = group("kv pair", kvs)
     put(kvs, kvin, twin)
     kv_pair_arrived()
-    row8 = lax.broadcasted_iota(jnp.int32, (8, 128), 0)
-    msgs[y, 0:16, :] = total + kvin[0:16, :]
-    msgs[y, 16:24, :] = jnp.where(row8 == core, fill, kvin[16:24, :])
+    msgs[y] = total + kvin[...]
     put, messages_arrived = group("messages", msgs.at[0:3])
     for d in (2, 3, 1):
         put(msgs.at[y], msgs.at[y], device(z, lax.rem(y + d, NY), core, x, h))
 
     cache_line_arrived()
+    length_line_arrived()
+    put, length_relay_arrived = group("length relay", fill.at[0:1])
+    put(fill.at[2:3], fill.at[3:4], twin)
     put, cache_relay_arrived = group("cache relay", kb.at[0:2])
     for buf in (kb, vb):
         put(buf.at[2], buf.at[3], twin)
+    length_twin_arrived()
     cache_twin_arrived()
-    messages_arrived()
+    length_relay_arrived()
     cache_relay_arrived()
 
     scale = LOG2E / math.sqrt(128.0)
     place = lax.broadcasted_iota(jnp.int32, (1, 512), 1).astype(F32)
-    bias, lengths = [], []
-    for chip in (y, keys_y):
-        pair = (msgs[chip, 16:17, :], msgs[chip, 17:18, :])
-        lengths += [jnp.where(core == 0, *pair), jnp.where(core == 0, *pair[::-1])]
-    for length in lengths:
-        filled = jnp.concatenate([length] * 4, axis=1)
+    bias = []
+    for slot in range(4):
+        filled = jnp.concatenate([fill[slot : slot + 1, :]] * 4, axis=1)
         bias.append(jnp.where(place < filled, 0.0, NEG))
     bias = jnp.concatenate(bias, axis=1)
     keys = kb[...].reshape(2048, 128)
     values = vb[...].reshape(2048, 128)
     diagonal = lax.broadcasted_iota(jnp.int32, (32, 128), 0) == lax.broadcasted_iota(jnp.int32, (32, 128), 1)
-    row16 = lax.broadcasted_iota(jnp.int32, (16, 128), 0)
 
     def attend(j, new):
         queries = qb[j]
         scores = dot_t(queries, keys) * scale + bias
         top = jnp.max(scores, axis=1, keepdims=True)
-        if new:
-            new_keys = jnp.concatenate([msgs[i, 0:16, :] for i in (0, 2)], axis=0).astype(BF16)
-            new_values = jnp.concatenate([msgs[i, 0:16, :] for i in (1, 3)], axis=0).astype(BF16)
-            key_at = lax.broadcasted_iota(jnp.int32, (256, 32), 1) + z * 32
-            row_at = lax.broadcasted_iota(jnp.int32, (256, 32), 0)
-            fresh = jnp.where(key_at <= row_at, dot_t(queries, new_keys) * scale, NEG)
-            top = jnp.maximum(top, jnp.max(fresh, axis=1, keepdims=True))
         weight = jnp.exp2(scores - top)
         sums = jnp.sum(weight, axis=1, keepdims=True)
         mixed = dot(weight.astype(BF16), values)
         if new:
-            weight = jnp.exp2(fresh - top)
-            sums = sums + jnp.sum(weight, axis=1, keepdims=True)
-            mixed = mixed + dot(weight.astype(BF16), new_values)
+            messages_arrived()
+            new_keys = jnp.concatenate([msgs[i] for i in (0, 2)], axis=0).astype(BF16)
+            new_values = jnp.concatenate([msgs[i] for i in (1, 3)], axis=0).astype(BF16)
+            key_at = lax.broadcasted_iota(jnp.int32, (256, 32), 1) + z * 32
+            row_at = lax.broadcasted_iota(jnp.int32, (256, 32), 0)
+            fresh = jnp.where(key_at <= row_at, dot_t(queries, new_keys) * scale, NEG)
+            raised = jnp.maximum(top, jnp.max(fresh, axis=1, keepdims=True))
+            shrink = jnp.exp2(top - raised)
+            weight = jnp.exp2(fresh - raised)
+            sums = sums * shrink + jnp.sum(weight, axis=1, keepdims=True)
+            mixed = mixed * shrink + dot(weight.astype(BF16), new_values)
+            top = raised
         shared = (mixed / sums).astype(BF16)
         level = top + jnp.log2(sums)
         for b in range(NZ):
             rows = slice(32 * b, 32 * b + 32)
-            po[j, b, 0:32, :] = shared[rows]
+            po[j, b] = shared[rows]
             line = jnp.sum(jnp.where(diagonal, level[rows], 0.0), axis=0, keepdims=True)
-            high = line.astype(BF16).astype(F32)
-            mid = (line - high).astype(BF16).astype(F32)
-            low = line - high - mid
-            po[j, b, 32:48, :] = jnp.where(row16 == 0, high, jnp.where(row16 == 1, mid, low)).astype(BF16)
+            pl_s[j, b : b + 1, :] = line
 
     put0, partials0_arrived = group("partials 0", pod.at[0, 0:7])
     put1, partials1_arrived = group("partials 1", pod.at[1])
+    putl0, levels0_arrived = group("levels 0", pl_d.at[0, 0:7])
+    putl1, levels1_arrived = group("levels 1", pl_d.at[1])
     heads1_arrived()
     attend(1, False)
     for d in (4, 3, 5, 2, 6, 1, 7, 0):
         to, dev = zdev(d, heads_y)
         put1(po.at[1, to], pod.at[1, z], dev)
+        putl1(pl_s.at[1, pl.ds(to, 1)], pl_d.at[1, pl.ds(z, 1)], dev)
     heads0_arrived()
     attend(0, True)
     for d in (4, 3, 5, 2, 6, 1, 7):
         to, dev = zdev(d)
         put0(po.at[0, to], pod.at[0, z], dev)
+        putl0(pl_s.at[0, pl.ds(to, 1)], pl_d.at[0, pl.ds(z, 1)], dev)
     pod[0, z] = po[0, z]
-    partials0_arrived()
-    partials1_arrived()
+    pl_d[0, pl.ds(z, 1), :] = pl_s[0, pl.ds(z, 1), :]
+    for arrived in (partials0_arrived, levels0_arrived, partials1_arrived, levels1_arrived):
+        arrived()
 
     levels, parts = [], []
     for j in range(2):
         for b in range(NZ):
-            rows = pod[j, b, 32:48, :].astype(F32)
-            line = rows[0:1] + rows[1:2] + rows[2:3]
-            spread = jnp.where(diagonal, jnp.broadcast_to(line, (32, 128)), 0.0)
+            spread = jnp.where(diagonal, jnp.broadcast_to(pl_d[j, b : b + 1, :], (32, 128)), 0.0)
             levels.append(jnp.sum(spread, axis=1, keepdims=True))
-            parts.append(pod[j, b, 0:32, :].astype(F32))
+            parts.append(pod[j, b].astype(F32))
     top = functools.reduce(jnp.maximum, levels)
     shares = [jnp.exp2(one - top) for one in levels]
     whole = functools.reduce(jnp.add, shares)
@@ -388,10 +392,11 @@
             vmem((4, 128, 256), BF16), vmem((4, 128, 128), BF16), vmem((2, 256, 256), BF16),
             vmem((4, 512, 128), BF16), vmem((4, 512, 128), BF16),
             vmem((2, 256, 128), F32), vmem((256, 128), F32), vmem((256, 128), F32),
-            vmem((24, 128), F32), vmem((24, 128), F32),
+            vmem((16, 128), F32), vmem((16, 128), F32), vmem((8, 128), F32),
             vmem((8, 32, 128), F32), vmem((8, 32, 128), F32), vmem((8, 16, 128), F32), vmem((8, 16, 128), F32),
-            vmem((2, 256, 128), BF16), vmem((4, 24, 128), F32),
-            vmem((2, 8, 48, 128), BF16), vmem((2, 8, 48, 128), BF16),
+            vmem((2, 256, 128), BF16), vmem((4, 16, 128), F32),
+            vmem((2, 8, 32, 128), BF16), vmem((2, 8, 32, 128), BF16),
+            vmem((2, 8, 128), F32), vmem((2, 8, 128), F32),
             vmem((2, 256, 256), BF16), vmem((2, 256, 128), BF16), vmem((16, 32, 128), BF16),
             dma((7,)), dma((len(GROUPS),)), dma((len(GROUPS),)), dma((8,)), dma((8,)), dma((4,)), dma((4,)),
             pltpu.SemaphoreType.REGULAR((5,)),

time: 62.6 us -> 61.8 us (0.987)
  Pallas kernels: 60.4 us -> 59.6 us
    pallas_call x1, Pallas kernels: 60.4 us -> 59.6 us  [per_device(): pl.pallas_call(kernel, out_shape=jax.ShapeDtypeStruct((32, 128), F32), in...]
where the time goes in v6:
time: 61.8 us; the launch traced here: 61.6 us
  Pallas kernels  59.6 us (96%)
  local copies, waits for them, and re-layouts  1.32 us (2%)
  between operations  0.66 us (1%)
    pallas_call x1, Pallas kernels, per_device(): pl.pallas_call(kernel, out_shape=jax.ShapeDtypeStruct((32, 128), F32), in...  59.6 us
    unnamed x1, local copies, waits for them, and re-layouts  1.32 us

profile of v6, /device:TPU:1, one launch (start us, length us, event | category | flops | bytes accessed | tf_op | source)
XLA Modules:
  0.0 61.6 jit_solution(13726853706696966532)
XLA Ops:
  0.7 59.6 %attention_block.1 = f32[32,128]{1,0:T(8,128)} custom-call(bf16[32,128]{1,0:T(8,128)(2,1)} %hid_ref.1, bf16[128,1024]{1,0:T(8,128)(2,1)} %wq_ref.1, bf16[128,128]{1,0:T(8,128)(2,1)} %wk_ref.1, bf16[128,128]{1,0:T(8,128)(2,1)} %wv_ref.1, bf16[1024,128]{1,0:T(8,128)(2,1)} %wo_ref.1, bf16[512,128]{1,0:T(8,128)(2,1)} %bitcast.2, bf16[512,128]{1,0:T(8,128)(2,1)} %bitcast.3, ...), custom_call_target="tpu_custom_call" | custom-call | flops 1000000000 | bytes 2000000 | tf_op jit(solution)/shard_map/attention_block/pallas_call | solution.py:385
  60.3 1.3 %copy.11 = f32[32,128]{1,0:T(8,128)} copy(f32[32,128]{1,0:T(8,128)} %attention_block.1) | data formatting | bytes 32768

commit v7 on v6

--- a/solution.py
+++ b/solution.py
@@ -91,9 +91,6 @@
         pltpu.make_async_copy(cv_ref, vb.at[0], loc.at[5]),
         pltpu.make_async_copy(wo_ref, wos, loc.at[6]),
     ]
-    for copy in local:
-        copy.start()
-
     barrier = pltpu.get_barrier_semaphore()
 
     def zdev(d, at_y=y):
@@ -109,6 +106,8 @@
     near += [zdev(1)[1], zdev(7)[1], twin]
     for dev in near:
         pl.semaphore_signal(barrier, inc=1, device_id=dev, device_id_type=MESH)
+    for copy in local:
+        copy.start()
     pl.semaphore_wait(barrier, len(near))
 
     def tell(i, d):
@@ -172,28 +171,13 @@
         to = lax.rem(y + d, NY)
         put(wkvs.at[to % 2], wkv.at[y], device(z, to, core, x, h))
 
-    query_weights_arrived()
     put, length_line_arrived = group("length line", fill.at[0:1])
     put(fill.at[0:1], fill.at[2:3], device(z, keys_y, core, x, h))
     put, cache_line_arrived = group("cache line", kb.at[0:2])
     for buf in (kb, vb):
         put(buf.at[0], buf.at[2], device(z, keys_y, core, x, h))
-    wqf = wq[...].reshape(512, 256)
-
-    def project(block):
-        rows = pl.ds(pl.multiple_of(block * 64, 64), 64)
-        both = dot(hs[rows, :], wqf)
-        yp[0, rows, :] = both[:, :128]
-        yp[1, rows, :] = both[:, 128:]
-
-    project(x)
-    for d in (1, 3, 2):
-        hidden_x(d, x_rows).wait_recv()
-        project(lax.rem(x + NX - d, NX))
-
-    put, pair_arrived = group("pair", yin)
-    put(yp.at[other], yin, twin)
-
+
+    query_weights_arrived()
     put, out_weights_arrived = group("out weights", wo.at[0])
     local[6].wait()
     for pair_core in range(2):
@@ -204,6 +188,22 @@
             there = wo.at[pair_core, pl.ds(128 * chip, 128)]
             put(wos.at[rows_of(heads_y)], there.at[:, pl.ds(128, 128)], device(z, heads_y, core, x, h))
             wo[pair_core, 128 * chip : 128 * chip + 128, 0:128] = wos[rows_of(y), :]
+
+    wqf = wq[...].reshape(512, 256)
+
+    def project(block):
+        rows = pl.ds(pl.multiple_of(block * 64, 64), 64)
+        both = dot(hs[rows, :], wqf)
+        yp[0, rows, :] = both[:, :128]
+        yp[1, rows, :] = both[:, 128:]
+
+    project(x)
+    for d in (1, 3, 2):
+        hidden_x(d, x_rows).wait_recv()
+        project(lax.rem(x + NX - d, NX))
+
+    put, pair_arrived = group("pair", yin)
+    put(yp.at[other], yin, twin)
 
     pair_arrived()
     for b in range(NZ):

time: 61.8 us -> 61.1 us (0.989)
    pallas_call x1, Pallas kernels: 59.6 us -> 59 us  [per_device(): pl.pallas_call(kernel, out_shape=jax.ShapeDtypeStruct((32, 128), F32), in...]
where the time goes in v7:
time: 61.1 us; the launch traced here: 60.9 us
  Pallas kernels  59 us (97%)
  local copies, waits for them, and re-layouts  1.32 us (2%)
  between operations  0.66 us (1%)
    pallas_call x1, Pallas kernels, per_device(): pl.pallas_call(kernel, out_shape=jax.ShapeDtypeStruct((32, 128), F32), in...  59 us
    unnamed x1, local copies, waits for them, and re-layouts  1.32 us

profile of v7, /device:TPU:1, one launch (start us, length us, event | category | flops | bytes accessed | tf_op | source)
XLA Modules:
  0.0 60.9 jit_solution(2189835246199868644)
XLA Ops:
  0.7 59.0 %attention_block.1 = f32[32,128]{1,0:T(8,128)} custom-call(bf16[32,128]{1,0:T(8,128)(2,1)} %hid_ref.1, bf16[128,1024]{1,0:T(8,128)(2,1)} %wq_ref.1, bf16[128,128]{1,0:T(8,128)(2,1)} %wk_ref.1, bf16[128,128]{1,0:T(8,128)(2,1)} %wv_ref.1, bf16[1024,128]{1,0:T(8,128)(2,1)} %wo_ref.1, bf16[512,128]{1,0:T(8,128)(2,1)} %bitcast.2, bf16[512,128]{1,0:T(8,128)(2,1)} %bitcast.3, ...), custom_call_target="tpu_custom_call" | custom-call | flops 1000000000 | bytes 2000000 | tf_op jit(solution)/shard_map/attention_block/pallas_call | solution.py:385
  59.6 1.3 %copy.11 = f32[32,128]{1,0:T(8,128)} copy(f32[32,128]{1,0:T(8,128)} %attention_block.1) | data formatting | bytes 32768

commit v8 on v7

--- a/solution.py
+++ b/solution.py
@@ -150,13 +150,17 @@
     for i, buf in enumerate((kb, vb)):
         local[4 + i].wait()
         put(buf.at[0], buf.at[1], twin)
-    for copy in local[2:4]:
-        copy.wait()
-    wkv[y] = wkvs[y % 2]
 
     for d in (1, 7, 2, 6):
         hidden_y(d).wait_recv()
         forward(d)
+    for copy in local[2:4]:
+        copy.wait()
+    put, kv_weights_arrived = group("kv weights", wkv.at[0:3])
+    for d in (2, 3, 1):
+        to = lax.rem(y + d, NY)
+        put(wkvs.at[to % 2], wkv.at[y], device(z, to, core, x, h))
+    wkv[y] = wkvs[y % 2]
     for i in range(2):
         pl.semaphore_wait(known.at[i], 1)
     tell(2, 1)
@@ -165,11 +169,6 @@
     for d in (3, 5, 4):
         hidden_y(d).wait_recv()
         forward(d)
-
-    put, kv_weights_arrived = group("kv weights", wkv.at[0:3])
-    for d in (2, 3, 1):
-        to = lax.rem(y + d, NY)
-        put(wkvs.at[to % 2], wkv.at[y], device(z, to, core, x, h))
 
     put, length_line_arrived = group("length line", fill.at[0:1])
     put(fill.at[0:1], fill.at[2:3], device(z, keys_y, core, x, h))
@@ -313,14 +312,14 @@
     attend(1, False)
     for d in (4, 3, 5, 2, 6, 1, 7, 0):
         to, dev = zdev(d, heads_y)
+        putl1(pl_s.at[1, pl.ds(to, 1)], pl_d.at[1, pl.ds(z, 1)], dev)
         put1(po.at[1, to], pod.at[1, z], dev)
-        putl1(pl_s.at[1, pl.ds(to, 1)], pl_d.at[1, pl.ds(z, 1)], dev)
     heads0_arrived()
     attend(0, True)
     for d in (4, 3, 5, 2, 6, 1, 7):
         to, dev = zdev(d)
+        putl0(pl_s.at[0, pl.ds(to, 1)], pl_d.at[0, pl.ds(z, 1)], dev)
         put0(po.at[0, to], pod.at[0, z], dev)
-        putl0(pl_s.at[0, pl.ds(to, 1)], pl_d.at[0, pl.ds(z, 1)], dev)
     pod[0, z] = po[0, z]
     pl_d[0, pl.ds(z, 1), :] = pl_s[0, pl.ds(z, 1), :]
     for arrived in (partials0_arrived, levels0_arrived, partials1_arrived, levels1_arrived):

time: 61.1 us -> 61.3 us (level)
  no operation moved by 1% of the time
where the time goes in v8:
time: 61.3 us; the launch traced here: 61.1 us
  Pallas kernels  59.2 us (97%)
  local copies, waits for them, and re-layouts  1.32 us (2%)
  between operations  0.66 us (1%)
    pallas_call x1, Pallas kernels, per_device(): pl.pallas_call(kernel, out_shape=jax.ShapeDtypeStruct((32, 128), F32), in...  59.2 us
    unnamed x1, local copies, waits for them, and re-layouts  1.32 us

profile of v8, /device:TPU:1, one launch (start us, length us, event | category | flops | bytes accessed | tf_op | source)
XLA Modules:
  0.0 61.1 jit_solution(7580329828394743573)
XLA Ops:
  0.7 59.2 %attention_block.1 = f32[32,128]{1,0:T(8,128)} custom-call(bf16[32,128]{1,0:T(8,128)(2,1)} %hid_ref.1, bf16[128,1024]{1,0:T(8,128)(2,1)} %wq_ref.1, bf16[128,128]{1,0:T(8,128)(2,1)} %wk_ref.1, bf16[128,128]{1,0:T(8,128)(2,1)} %wv_ref.1, bf16[1024,128]{1,0:T(8,128)(2,1)} %wo_ref.1, bf16[512,128]{1,0:T(8,128)(2,1)} %bitcast.2, bf16[512,128]{1,0:T(8,128)(2,1)} %bitcast.3, ...), custom_call_target="tpu_custom_call" | custom-call | flops 1000000000 | bytes 2000000 | tf_op jit(solution)/shard_map/attention_block/pallas_call | solution.py:384
  59.8 1.3 %copy.11 = f32[32,128]{1,0:T(8,128)} copy(f32[32,128]{1,0:T(8,128)} %attention_block.1) | data formatting | bytes 32768
